TPU v7x, 32 devices: a whole 2x2x4 slice. The times are simulated.
32 devices in a mesh: gx: 16 (over z, x, core), gy: 2 (over y).
Axes of the slice: x: 2, y: 2, z: 4, core: 2. Of those that a mesh axis runs over, the one named last changes fastest.
Arguments:
- labels: int32 [1, 2048, 2048], P(None, 'gx', 'gy'), may hold values from 0 to 2
- damage: float32 [1, 2048, 2048], P(None, 'gx', 'gy'), may hold values from -6 to 6
- opening: float32 [1, 2048, 2048], P(None, 'gx', 'gy'), may hold values from -6 to 6
- strain: float32 [3, 1, 2048, 2048], P(None, None, 'gx', 'gy'), may hold values from -6 to 6
Outputs:
- correlations: float32 [21, 1, 2048, 2048], P(None, None, 'gx', 'gy')
All inputs are finite; a program needn't handle non-finite values.
Results may differ from a plain program's by a relative error of at most 0.00013.
Values sent between devices are 32-bit elements; how exact they have to be, the bound alone decides.
A program may use at most 192 MiB of HBM per device.

v0:
```python
import math

import jax
import jax.numpy as jnp
from jax import lax
from jax.sharding import PartitionSpec as P

GRID = 2048


HIGHEST = lax.Precision.HIGHEST


def phase_table(row_count, col_count, length, orient):
    row_index = lax.broadcasted_iota(jnp.int32, (row_count, col_count), 0)
    col_index = lax.broadcasted_iota(jnp.int32, (row_count, col_count), 1)
    angles = (row_index * col_index % length).astype(jnp.float32) * (2.0 * math.pi / length)
    return (jnp.cos(angles), orient * jnp.sin(angles))


def contract(stacked, factors, pattern):
    cosine, sine_part = factors

    def product(values, matrix):
        return jnp.einsum(
            pattern, values, matrix, precision=HIGHEST, preferred_element_type=jnp.float32
        )

    if stacked.shape[0] == 1:
        return jnp.stack([product(stacked[0], cosine), product(stacked[0], sine_part)])
    real_part, imag_part = (stacked[0], stacked[1])
    return jnp.stack(
        [
            product(real_part, cosine) - product(imag_part, sine_part),
            product(real_part, sine_part) + product(imag_part, cosine),
        ]
    )


def rotate(stacked, factors):
    cosine, sine_part = factors
    real_part, imag_part = (stacked[0], stacked[1])
    return jnp.stack(
        [real_part * cosine - imag_part * sine_part, real_part * sine_part + imag_part * cosine]
    )


def y_transform(stacked, orient):
    members, item_count, line_count, length = stacked.shape
    minor_size = 128
    major_size = length // minor_size
    blocks = stacked.reshape(members, item_count, line_count, major_size, minor_size)
    if orient < 0:
        blocks = contract(
            blocks, phase_table(major_size, major_size, major_size, orient), "bmuv,ku->bmkv"
        )
        blocks = rotate(blocks, phase_table(major_size, minor_size, length, orient))
        blocks = contract(
            blocks, phase_table(minor_size, minor_size, minor_size, orient), "bmkv,vn->bmkn"
        )
    else:
        blocks = contract(
            blocks, phase_table(minor_size, minor_size, minor_size, orient), "bmkn,nv->bmkv"
        )
        blocks = rotate(blocks, phase_table(major_size, minor_size, length, orient))
        blocks = contract(
            blocks, phase_table(major_size, major_size, major_size, orient), "bmkv,ku->bmuv"
        )
    return blocks.reshape(2, item_count, line_count, length)


def x_transform(stacked, orient):
    members, item_count, row_count, col_count = stacked.shape
    devices = lax.axis_size("gx")
    piece_size = row_count * col_count // devices
    device_index = lax.axis_index("gx")
    grid_size = row_count * devices
    frequency = lax.broadcasted_iota(jnp.int32, (devices, piece_size), 0)
    offset = lax.broadcasted_iota(jnp.int32, (devices, piece_size), 1)
    position = (device_index * piece_size + offset) // col_count
    angles = (position * frequency % grid_size).astype(jnp.float32) * (2.0 * math.pi / grid_size)
    twiddle = (jnp.cos(angles), orient * jnp.sin(angles))
    square = phase_table(devices, devices, devices, orient)
    if orient > 0:
        stacked = contract(
            stacked, phase_table(row_count, row_count, row_count, orient), "bkp,kr->brp"
        )

    def spread_work(received):
        if orient < 0:
            return rotate(contract(received, square, "bal,ka->bkl"), twiddle)
        return contract(rotate(received, twiddle), square, "bkl,ka->bal")

    spread = spread_work(
        lax.all_to_all(
            stacked.reshape(stacked.shape[0], item_count, devices, piece_size),
            "gx",
            split_axis=2,
            concat_axis=2,
            tiled=True,
        )
    )

    def collect_work(received):
        shaped = received.reshape(received.shape[0], received.shape[1], row_count, col_count)
        if orient < 0:
            return contract(
                shaped, phase_table(row_count, row_count, row_count, orient), "brp,kr->bkp"
            )
        return shaped

    return collect_work(lax.all_to_all(spread, "gx", split_axis=2, concat_axis=3, tiled=True))


def pencil_open(stacked, orient):
    return y_transform(
        lax.all_to_all(stacked, "gy", split_axis=2, concat_axis=3, tiled=True), orient
    )


def pencil_close(stacked):
    return lax.all_to_all(stacked, "gy", split_axis=3, concat_axis=2, tiled=True)


def pair_spectra(spectra, field_count, planes):
    members, item_count, line_count, length = spectra.shape
    shaped = spectra.reshape(2, field_count, planes, line_count, length)
    real_part, imag_part = (shaped[0], shaped[1])
    crosses = []
    for left_field in range(field_count):
        for right_field in range(left_field, field_count):
            crosses.append(
                (
                    real_part[left_field] * real_part[right_field]
                    + imag_part[left_field] * imag_part[right_field],
                    real_part[left_field] * imag_part[right_field]
                    - imag_part[left_field] * real_part[right_field],
                )
            )
    nothing = jnp.zeros_like(real_part[0])
    crosses.append((nothing, nothing))
    packed_real = []
    packed_imag = []
    for number in range(0, len(crosses), 2):
        even_pair = crosses[number]
        odd_pair = crosses[number + 1]
        packed_real.append(even_pair[0] - odd_pair[1])
        packed_imag.append(even_pair[1] + odd_pair[0])
    return jnp.stack([jnp.stack(packed_real), jnp.stack(packed_imag)]).reshape(
        2, -1, line_count, length
    )


def local(labels, damage, opening, strain):
    phase_field = labels.astype(jnp.float32) - 1.0
    fields = jnp.concatenate([phase_field[None], damage[None], opening[None], strain], axis=0)
    field_count, planes, row_count, col_count = fields.shape
    stacked = fields.reshape(1, field_count * planes, row_count, col_count)
    spectra = pencil_open(x_transform(stacked, -1.0), -1.0)
    packed = pair_spectra(spectra, field_count, planes)
    result = x_transform(pencil_close(y_transform(packed, 1.0)), 1.0)
    pair_count = field_count * (field_count + 1) // 2
    shaped = result.reshape(2, -1, planes, row_count, col_count)
    alternated = jnp.stack([shaped[0], shaped[1]], axis=1).reshape(-1, planes, row_count, col_count)
    scale = 1.0 / (float(GRID) * float(GRID) * float(GRID))
    return alternated[:pair_count] * scale


def solution(mesh):
    in_specs = (
        P(None, "gx", "gy"),
        P(None, "gx", "gy"),
        P(None, "gx", "gy"),
        P(None, None, "gx", "gy"),
    )
    out_specs = P(None, None, "gx", "gy")
    return jax.shard_map(local, mesh=mesh, in_specs=in_specs, out_specs=out_specs, check_vma=False)
```

profile of v0, /device:TPU:0, one launch (start us, length us, event | category | flops | bytes accessed | tf_op | source)
XLA Modules:
  0.0 1609.4 jit_solution(3971489491676914424)
XLA Ops:
  21.0 56.0 %all-to-all-done = f32[1,6,16,8192]{3,0,1,2:T(1,128)S(1)} async-done(((f32[1,6,16,8192]{3,0,1,2:T(1,128)}), f32[1,6,16,8192]{3,0,1,2:T(1,128)S(1)}, u32[]{:S(2)}, u32[]{:S(2)}) %all-to-all-start) | async-done | bytes 3145760 | tf_op jit(solution)/shard_map/all_to_all | solution.py:95
  87.1 8.0 copy.183
  95.0 152.7 %all_to_all.58 = f32[2,6,16,8192]{3,0,1,2:T(2,128)} all-to-all(f32[2,6,16,8192]{3,0,1,2:T(2,128)} %copy.183), channel_id=1, replica_groups=mesh['gx'=16,'gy'=2] {'gx'}, dimensions={2} | all-to-all | bytes 12582912 | tf_op jit(solution)/shard_map/all_to_all | solution.py:112
  247.8 12.9 fusion.272
  308.0 70.9 %all-to-all-done.2 = f32[2,6,128,1024]{3,0,1,2:T(2,128)} async-done(((f32[2,6,128,1024]{3,0,1,2:T(2,128)}), f32[2,6,128,1024]{3,0,1,2:T(2,128)}, u32[]{:S(2)}, u32[]{:S(2)}) %all-to-all-start.2) | async-done | bytes 6291488 | tf_op jit(solution)/shard_map/all_to_all | solution.py:117
  379.0 7.6 copy.284
  480.5 13.6 add_bitcast_fusion.1
  501.2 10.4 pad_maximum_fusion
  511.7 31.3 %copy.204 = f32[2,11,64,2048]{2,0,1,3:T(2,128)} copy(f32[2,11,64,2048]{3,2,1,0:T(8,128)} %pad_maximum_fusion) | data formatting | bytes 23068672 | tf_op jit(solution)/shard_map/stack | solution.py:32
  543.0 41.2 %reshape.957 = f32[2,1,1441792]{2,1,0:T(1,128)} reshape(f32[2048,11,2,64]{3,2,1,0:T(2,128)} %bitcast.246) | data formatting | bytes 23068672
  584.2 140.1 %all_to_all.59 = f32[2,1,1441792]{2,1,0:T(1,128)} all-to-all(f32[2,1,1441792]{2,1,0:T(1,128)} %reshape.957), channel_id=1, replica_groups=mesh['gx'=16,'gy'=2] {'gy'}, dimensions={0} | all-to-all | bytes 23068672 | tf_op jit(solution)/shard_map/all_to_all | solution.py:122
  724.8 40.1 %reduce = f32[2,1441792]{1,0:T(2,128)} reduce(f32[2,1,1441792]{2,1,0:T(1,128)} %all_to_all.59, f32[]{:T(128)} %broadcast.613), dimensions={1}, to_apply=%all_to_all.47.reduce_sub_computation | reduce | bytes 23068676 | tf_op jit(solution)/shard_map/all_to_all | solution.py:122
  764.9 45.6 %reshape.958 = f32[2048,11,2,64]{3,2,1,0:T(2,128)} reshape(f32[2,1441792]{1,0:T(2,128)} %reduce) | data formatting | bytes 23068672
  810.4 31.4 %copy.205 = f32[2,11,64,2,1024]{4,2,3,1,0:T(8,128)} copy(f32[2,11,64,2,1024]{2,0,1,4,3:T(2,128)} %bitcast.247) | data formatting | bytes 23068672 | tf_op jit(solution)/shard_map/all_to_all | solution.py:122
  841.9 8.8 fusion.270
  850.7 10.3 fusion.55
  883.0 9.3 copy.206
  914.3 10.4 pad_maximum_fusion.1
  924.7 254.2 %all_to_all.60 = f32[2,11,16,8192]{3,0,1,2:T(2,128)S(1)} all-to-all(f32[2,11,16,8192]{3,0,1,2:T(2,128)S(1)} %pad_maximum_fusion.1), channel_id=1, replica_groups=mesh['gx'=16,'gy'=2] {'gx'}, dimensions={2} | all-to-all | bytes 23068672 | tf_op jit(solution)/shard_map/all_to_all | solution.py:95
  1178.9 12.3 fusion.269
  1191.2 14.2 fusion.26
  1205.4 14.4 fusion.25
  1219.8 15.4 fusion.2
  1235.1 16.3 %fusion.1 = f32[1,11,16,8192]{3,2,1,0:T(8,128)} fusion(f32[16,11,8192]{2,0,1:T(8,128)} %fusion.25, f32[1,11,16,8192]{3,0,1,2:T(1,128)S(1)} %get-tuple-element.10, f32[1,11,16,8192]{3,0,1,2:T(1,128)S(1)} %get-tuple-element.9, f32[16,8192]{1,0:T(8,128)S(1)} %copy-done.7, f32[16,8192]{1,0:T(8,128)S(1)} %copy-done.6), kind=kOutput, calls=%fused_computation.7 | convolution fusion | flops 282594816 | bytes 24117248 | tf_op jit(solution)/shard_map/bkl,ka->bal/dot_general | solution.py:25
  1251.4 8.3 pad_maximum_fusion.2
  1259.7 19.3 %copy.210 = f32[2,11,16,8192]{3,0,1,2:T(2,128)S(1)} copy(f32[2,11,16,8192]{3,2,1,0:T(8,128)} %pad_maximum_fusion.2) | data formatting | bytes 23068672 | tf_op jit(solution)/shard_map/stack | solution.py:32
  1279.0 255.5 %all_to_all.61 = f32[2,11,16,8192]{3,0,1,2:T(2,128)S(1)} all-to-all(f32[2,11,16,8192]{3,0,1,2:T(2,128)S(1)} %copy.210), channel_id=1, replica_groups=mesh['gx'=16,'gy'=2] {'gx'}, dimensions={2} | all-to-all | bytes 23068672 | tf_op jit(solution)/shard_map/all_to_all | solution.py:112
  1534.6 9.9 fusion.268
  1558.9 10.0 copy.212
  1576.1 11.1 pad_maximum_fusion.3
  1587.2 10.9 copy.213
  1598.2 11.0 fusion
  (108 shorter events, 245.1 us)
Async XLA Ops:
  10.2 66.7 %all-to-all-start = ((f32[1,6,16,8192]{3,0,1,2:T(1,128)}), f32[1,6,16,8192]{3,0,1,2:T(1,128)S(1)}, u32[]{:S(2)}, u32[]{:S(2)}) async-start(f32[1,6,16,8192]{3,0,1,2:T(1,128)} %copy.179), calls=%async_computation | async-start | bytes 6291456 | tf_op jit(solution)/shard_map/all_to_all | solution.py:95
  76.9 4.4 copy-start.5
  76.9 4.4 copy-start.11
  267.5 9.5 copy-start.8
  284.2 5.3 copy-start.9
  301.4 77.5 %all-to-all-start.2 = ((f32[2,6,128,1024]{3,0,1,2:T(2,128)}), f32[2,6,128,1024]{3,0,1,2:T(2,128)}, u32[]{:S(2)}, u32[]{:S(2)}) async-start(f32[2,6,128,1024]{3,0,1,2:T(2,128)} %copy.190), calls=%async_computation.2 | async-start | bytes 12582912 | tf_op jit(solution)/shard_map/all_to_all | solution.py:117
  409.9 5.2 copy-start.10
  449.6 17.1 %copy-start = (f32[11,64,16,128]{3,2,1,0:T(8,128)}, f32[11,64,16,128]{3,2,1,0:T(8,128)S(1)}, u32[]{:S(2)}) copy-start(f32[11,64,16,128]{3,2,1,0:T(8,128)S(1)} %convolution_subtract_fusion.1) | copy-start | bytes 17301508
  454.5 12.2 copy-start.1
  850.7 17.6 %copy-start.2 = (f32[1,11,2,64,1024]{4,3,2,1,0:T(8,128)}, f32[1,11,2,64,1024]{4,3,2,1,0:T(8,128)S(1)}, u32[]{:S(2)}) copy-start(f32[1,11,2,64,1024]{4,3,2,1,0:T(8,128)S(1)} %get-tuple-element.11) | copy-start | bytes 17301508
  850.7 10.3 copy-start.3
  875.9 16.4 %slice-start = ((s8[5767168]{0:T(1024)(128)(4,1)}), s8[1572864]{0:T(1024)(128)(4,1)S(1)}, s32[]{:S(2)}) async-start(s8[5767168]{0:T(1024)(128)(4,1)} %bitcast.249), calls=%async_computation.6 | async-start | bytes 3145728
  883.0 9.3 slice-start.1
  883.0 9.3 copy-start.4
  899.8 14.5 slice-start.2
  906.9 7.3 slice-start.3
  1178.9 12.3 copy-start.6
  1178.9 12.3 copy-start.7
where the time goes:
time: 1620 us; the launch traced here: 1610 us
  blocking collectives  803 us (50%)
  local copies, waits for them, and re-layouts  361 us (22%)
  matrix products  203 us (13%)
  waiting for transfers between devices  127 us (8%)
  other arithmetic  101 us (6%)
    all_to_all x2, blocking collectives, x_transform(): lax.all_to_all(spread, 'gx', split_axis=2, concat_axis=3, tiled=True)  408 us
    all_to_all x1, blocking collectives, x_transform(): lax.all_to_all(stacked.reshape(stacked.shape[0], item_count, devices, pie...  254 us
    dot_general x30, matrix products, product(): jnp.einsum(pattern, values, matrix, precision=HIGHEST, preferred_element_...  203 us
    all_to_all x1, blocking collectives, pencil_close(): lax.all_to_all(stacked, 'gy', split_axis=3, concat_axis=2, tiled=True)  140 us
    another operation x9, local copies, waits for them, and re-layouts, contract(): jnp.stack([product(real_part, cosine) - product(imag_part, sine_part), pr...  103 us
    unnamed x34, local copies, waits for them, and re-layouts  86.8 us
    all_to_all x1, waiting for transfers between devices, pencil_open(): lax.all_to_all(stacked, 'gy', split_axis=2, concat_axis=3, tiled=True)  70.9 us
    all_to_all x1, waiting for transfers between devices, x_transform(): lax.all_to_all(stacked.reshape(stacked.shape[0], item_count, devices, pie...  56 us
  transfers between devices with their start and end apart: 2, of which 2 were waited for; matrix products, arithmetic and copies ran while one was open for 0% of the time, Pallas kernels for 0%

commit v1 on v0

--- a/solution.py
+++ b/solution.py
@@ -1,8 +1,13 @@
+import functools
 import math
 
 import jax
 import jax.numpy as jnp
+import ml_dtypes
+import numpy as np
 from jax import lax
+from jax.experimental import pallas as pl
+from jax.experimental.pallas import tpu as pltpu
 from jax.sharding import PartitionSpec as P
 
 GRID = 2048
@@ -151,7 +156,7 @@
     )
 
 
-def local(labels, damage, opening, strain):
+def plain_local(labels, damage, opening, strain):
     phase_field = labels.astype(jnp.float32) - 1.0
     fields = jnp.concatenate([phase_field[None], damage[None], opening[None], strain], axis=0)
     field_count, planes, row_count, col_count = fields.shape
@@ -166,6 +171,380 @@
     return alternated[:pair_count] * scale
 
 
+RADIX = 8
+PART = GRID // RADIX
+FIELD_COUNT = 6
+KEEP = 32
+ROOT = math.sqrt(0.5)
+PAIRS = [(i, j) for i in range(FIELD_COUNT) for j in range(i, FIELD_COUNT)]
+CHUNKS = ((0, 4), (4, 8), (8, 11))
+VMEM_BYTES = 56 * 1024 * 1024
+
+
+def split_table(table):
+    high = table.astype(np.float32).astype(ml_dtypes.bfloat16)
+    low = (table - high.astype(np.float64)).astype(np.float32).astype(ml_dtypes.bfloat16)
+    return np.stack([high, low])
+
+
+def angle_table(first):
+    b = np.arange(PART)[:, None]
+    k2 = np.arange(PART)[None, :]
+    return 2.0 * np.pi * ((b * (first + RADIX * k2)) % GRID) / GRID
+
+
+def lane_order(values_real, values_imag):
+    rows, count = values_real.shape
+    both = np.stack([values_real.reshape(rows, -1, KEEP), values_imag.reshape(rows, -1, KEEP)], axis=2)
+    return both.reshape(rows, 2 * count)
+
+
+@functools.lru_cache(maxsize=None)
+def tables():
+    half = PART // 2
+    small, large, small_back, large_back = [], [], [], []
+    for first in (0, 4):
+        angle = angle_table(first)[:, :half]
+        cosine, sine = np.cos(angle), np.sin(angle)
+        forward_imag = -sine
+        back_real, back_imag = 2.0 * cosine, -2.0 * sine
+        if first == 0:
+            alternating = np.cos(np.pi * np.arange(PART))
+            forward_imag[:, 0] = alternating
+            back_real[:, 0] = 1.0
+            back_imag[:, 0] = alternating
+        small.append(lane_order(cosine, forward_imag))
+        small_back.append(lane_order(back_real, back_imag).T)
+    for first in (1, 2, 3):
+        angle = angle_table(first)
+        cosine, sine = np.cos(angle), np.sin(angle)
+        large.append(np.concatenate([lane_order(cosine, -sine), lane_order(sine, cosine)], axis=0))
+        large_back.append(
+            2.0
+            * np.concatenate([lane_order(cosine, -sine).T, lane_order(sine, cosine).T], axis=1)
+        )
+    scale = 1.0 / (float(GRID) * float(GRID) * float(GRID))
+    across, across_back = [], []
+    for first in range(RADIX):
+        angle = angle_table(first)
+        cosine, sine = np.cos(angle), np.sin(angle)
+        across.append(np.concatenate([cosine.T, sine.T], axis=1))
+        across_back.append(np.concatenate([cosine, -sine], axis=1))
+    return tuple(
+        split_table(np.stack(group))
+        for group in (
+            small,
+            large,
+            [scale * table for table in small_back],
+            [scale * table for table in large_back],
+            across,
+            across_back,
+        )
+    )
+
+
+def halves(values):
+    high = values.astype(jnp.bfloat16)
+    low = (values - high.astype(jnp.float32)).astype(jnp.bfloat16)
+    return high, low
+
+
+def dot(left, right):
+    return jnp.dot(left, right, preferred_element_type=jnp.float32)
+
+
+def times_table(values, table_high, table_low):
+    high, low = halves(values)
+    return dot(high, table_high) + (dot(low, table_high) + dot(high, table_low))
+
+
+def table_times(table_high, table_low, values):
+    high, low = halves(values)
+    return dot(table_high, high) + (dot(table_high, low) + dot(table_low, high))
+
+
+def lane_mask(shape, period, first):
+    return lax.broadcasted_iota(jnp.int32, shape, 1) % period < first
+
+
+def minus_i(values):
+    real_lane = lane_mask(values.shape, 2 * KEEP, KEEP)
+    width = values.shape[1]
+    return jnp.where(
+        real_lane, pltpu.roll(values, width - KEEP, 1), -pltpu.roll(values, KEEP, 1)
+    )
+
+
+def eight(parts, turn):
+    e = [parts[a] + parts[a + 4] for a in range(4)]
+    d = [parts[a] - parts[a + 4] for a in range(4)]
+    even, odd = e[0] + e[2], e[1] + e[3]
+    twist = turn(e[1] - e[3])
+    flat = e[0] - e[2]
+    cross = turn(d[2])
+    near, far = d[0] + cross, d[0] - cross
+    span = turn(d[1] + d[3])
+    gap = d[1] - d[3]
+    first, third = ROOT * (span + gap), ROOT * (span - gap)
+    return [
+        even + odd,
+        near + first,
+        flat + twist,
+        far + third,
+        even - odd,
+        near - first,
+        flat - twist,
+        far - third,
+    ]
+
+
+def rows_kernel(x_ref, small_ref, large_ref, out_ref, wide):
+    parts_count, fields, rows, cols = x_ref.shape
+    per = cols // PART
+    count = fields * rows
+
+    def part(a):
+        return x_ref[a // per, :, :, (a % per) * PART : (a % per + 1) * PART].reshape(count, PART)
+
+    s = [part(a) for a in range(RADIX)]
+    e = [s[a] + s[a + 4] for a in range(4)]
+    d = [s[a] - s[a + 4] for a in range(4)]
+    even, odd = e[0] + e[2], e[1] + e[3]
+    gap, both = ROOT * (d[1] - d[3]), ROOT * (d[1] + d[3])
+    wide[:, 0:PART] = times_table(even + odd, small_ref[0, 0], small_ref[1, 0])
+    wide[:, PART : 2 * PART] = times_table(even - odd, small_ref[0, 1], small_ref[1, 1])
+    complexes = [
+        (d[0] + gap, -d[2] - both),
+        (e[0] - e[2], e[3] - e[1]),
+        (d[0] - gap, d[2] - both),
+    ]
+    for n, (real_part, imag_part) in enumerate(complexes):
+        wide[:, 2 * PART * (n + 1) : 2 * PART * (n + 2)] = times_table(
+            jnp.concatenate([real_part, imag_part], axis=1), large_ref[0, n], large_ref[1, n]
+        )
+    low_lanes = lane_mask((rows, 4 * KEEP), 4 * KEEP, 2 * KEEP)
+    for pair in range(fields // 2):
+        for u in range(GRID // (4 * KEEP)):
+            lanes = slice(4 * KEEP * u, 4 * KEEP * (u + 1))
+            one = wide[2 * pair * rows : (2 * pair + 1) * rows, lanes]
+            two = wide[(2 * pair + 1) * rows : (2 * pair + 2) * rows, lanes]
+            out_ref[2 * u, pair] = jnp.where(low_lanes, one, pltpu.roll(two, 2 * KEEP, 1))
+            out_ref[2 * u + 1, pair] = jnp.where(low_lanes, pltpu.roll(one, 2 * KEEP, 1), two)
+
+
+def columns_kernel(special_ref, x_ref, across_ref, main_ref, extra_ref, mixed):
+    devices, groups, rows, lanes = x_ref.shape
+    special = special_ref[0] == 0
+    step = 32
+
+    @pl.loop(0, PART // step)
+    def _(piece):
+        for group in range(groups):
+            parts = []
+            extras = []
+            for a in range(RADIX):
+                start = a * PART + piece * step
+                value = x_ref[start // rows, group, pl.ds(pl.multiple_of(start % rows, step), step), :]
+                lane = lax.broadcasted_iota(jnp.int32, value.shape, 1) % (2 * KEEP)
+                extras.append(
+                    jnp.where(
+                        jnp.logical_and(lane == 0, special), pltpu.roll(value, lanes - KEEP, 1), 0.0
+                    )
+                )
+                parts.append(jnp.where(jnp.logical_and(lane == KEEP, special), 0.0, value))
+            where = pl.ds(pl.multiple_of(piece * step, step), step)
+            for k1, value in enumerate(eight(parts, minus_i)):
+                mixed[k1, where, group * lanes : (group + 1) * lanes] = value
+            for k1, value in enumerate(eight(extras, minus_i)):
+                mixed[k1, where, (groups + group) * lanes : (groups + group + 1) * lanes] = value
+
+    @pl.loop(0, RADIX)
+    def _(k1):
+        value = mixed[k1]
+        both = jnp.concatenate([value, minus_i_wide(value)], axis=0)
+        result = table_times(across_ref[0, k1], across_ref[1, k1], both)
+        main_ref[k1] = result[:, : groups * lanes]
+        extra_ref[k1] = result[:, groups * lanes :]
+
+
+def minus_i_wide(values):
+    width = 4 * KEEP
+    return jnp.concatenate(
+        [minus_i(values[:, start : start + width]) for start in range(0, values.shape[1], width)],
+        axis=1,
+    )
+
+
+def pairs_kernel(numbers, main_ref, extra_ref, back_ref, out_ref, spread):
+    lanes = 4 * KEEP
+    tile = 32
+
+    def forms(ref, k1, rows, field):
+        group, side = field // 2, field % 2
+        value = ref[k1, rows, group * lanes : (group + 1) * lanes]
+        shape = value.shape
+        turned = pltpu.roll(value, 2 * KEEP, 1)
+        low = lane_mask(shape, lanes, 2 * KEEP)
+        full = jnp.where(low, value, turned) if side == 0 else jnp.where(low, turned, value)
+        forward, backward = pltpu.roll(full, lanes - KEEP, 1), pltpu.roll(full, KEEP, 1)
+        real_lane = lane_mask(shape, 2 * KEEP, KEEP)
+        real_part = jnp.where(real_lane, full, backward)
+        imag_part = jnp.where(real_lane, forward, full)
+        turned_part = jnp.where(real_lane, forward, -backward)
+        return real_part, imag_part, full, turned_part
+
+    used = [PAIRS[n] for q in numbers for n in (2 * q, 2 * q + 1) if n < len(PAIRS)]
+    fields = sorted({f for pair in used for f in pair})
+
+    @pl.loop(0, RADIX)
+    def _(k1):
+        @pl.loop(0, PART // tile)
+        def _(piece):
+            rows = pl.ds(pl.multiple_of(piece * tile, tile), tile)
+            main = {f: forms(main_ref, k1, rows, f) for f in fields}
+            extra = {f: forms(extra_ref, k1, rows, f) for f in fields}
+            low = lane_mask((tile, lanes), lanes, 2 * KEEP)
+
+            def cross(n):
+                i, j = PAIRS[n]
+                value = main[i][0] * main[j][2] + main[i][1] * main[j][3]
+                return value + (extra[i][1] * extra[j][2] - extra[i][0] * extra[j][3])
+
+            for place, q in enumerate(numbers):
+                one = cross(2 * q)
+                two = cross(2 * q + 1) if 2 * q + 1 < len(PAIRS) else jnp.zeros_like(one)
+                value = jnp.where(low, one, two)
+                spread[k1, rows, place * lanes : (place + 1) * lanes] = value
+
+        value = spread[k1]
+        both = jnp.concatenate([value, minus_i_wide(value)], axis=0)
+        spread[k1] = table_times(back_ref[0, k1], back_ref[1, k1], both)
+
+    block = out_ref.shape[2]
+
+    @pl.loop(0, PART // tile)
+    def _(piece):
+        rows = pl.ds(pl.multiple_of(piece * tile, tile), tile)
+        for place in range(len(numbers)):
+            parts = [
+                spread[k1, rows, place * lanes : (place + 1) * lanes] for k1 in range(RADIX)
+            ]
+            for a, value in enumerate(eight(parts, lambda v: -minus_i(v))):
+                start = a * PART + piece * tile
+                out_ref[
+                    start // block, place, pl.ds(pl.multiple_of(start % block, tile), tile), :
+                ] = value
+
+
+def back_kernel(pair_count, x_ref, small_ref, large_ref, out_ref, wide):
+    devices, groups, rows, lanes = x_ref.shape
+    cols = out_ref.shape[3]
+    per = cols // PART
+    low_lanes = lane_mask((rows, lanes), lanes, 2 * KEEP)
+    for place in range(pair_count):
+        group, side = place // 2, place % 2
+        for u in range(devices // 2):
+            one, two = x_ref[2 * u, group], x_ref[2 * u + 1, group]
+            if side == 0:
+                value = jnp.where(low_lanes, one, pltpu.roll(two, 2 * KEEP, 1))
+            else:
+                value = jnp.where(low_lanes, pltpu.roll(one, 2 * KEEP, 1), two)
+            wide[place * rows : (place + 1) * rows, lanes * u : lanes * (u + 1)] = value
+    for place in range(pair_count):
+        here = slice(place * rows, (place + 1) * rows)
+        u0 = times_table(wide[here, 0:PART], small_ref[0, 0], small_ref[1, 0])
+        u4 = times_table(wide[here, PART : 2 * PART], small_ref[0, 1], small_ref[1, 1])
+        us = []
+        for n in range(3):
+            value = times_table(
+                wide[here, 2 * PART * (n + 1) : 2 * PART * (n + 2)], large_ref[0, n], large_ref[1, n]
+            )
+            us.append((value[:, :PART], value[:, PART:]))
+        (u1r, u1i), (u2r, u2i), (u3r, u3i) = us
+        even, odd = u0 + u4, u0 - u4
+        sums, gaps = even + u2r, even - u2r
+        lefts, rights = odd - u2i, odd + u2i
+        p0, p2 = u1r + u3r, u3i - u1i
+        p1, p3 = ROOT * ((u1r - u1i) - (u3r + u3i)), ROOT * ((u3r - u3i) - (u1r + u1i))
+        results = [
+            sums + p0, lefts + p1, gaps + p2, rights + p3,
+            sums - p0, lefts - p1, gaps - p2, rights - p3,
+        ]
+        for a, value in enumerate(results):
+            out_ref[a // per, place, :, (a % per) * PART : (a % per + 1) * PART] = value
+
+
+def call(body, shapes, scratch, in_specs=None, operands=()):
+    count = len(operands)
+    vmem = pl.BlockSpec(memory_space=pltpu.VMEM)
+    return pl.pallas_call(
+        body,
+        out_shape=[jax.ShapeDtypeStruct(shape, jnp.float32) for shape in shapes],
+        in_specs=in_specs or [vmem] * count,
+        out_specs=[vmem] * len(shapes),
+        scratch_shapes=[pltpu.VMEM(shape, jnp.float32) for shape in scratch],
+        compiler_params=pltpu.CompilerParams(vmem_limit_bytes=VMEM_BYTES),
+    )(*operands)
+
+
+def pencil_local(labels, damage, opening, strain):
+    small, large, small_back, large_back, across, across_back = [jnp.asarray(t) for t in tables()]
+    phase_field = labels.astype(jnp.float32) - 1.0
+    fields = jnp.concatenate([phase_field, damage, opening, strain[:, 0]], axis=0)
+    field_count, row_count, cols = fields.shape
+    sides = lax.axis_size("gy")
+    devices = lax.axis_size("gx") * sides
+    rows = row_count // sides
+    sent = jnp.transpose(fields.reshape(field_count, sides, rows, cols), (1, 0, 2, 3))
+    lines = lax.all_to_all(sent, "gy", split_axis=0, concat_axis=0)
+    groups = field_count // 2
+    lanes = 4 * KEEP
+    (packed,) = call(
+        rows_kernel,
+        [(devices, groups, rows, lanes)],
+        [(field_count * rows, GRID)],
+        operands=(lines, small, large),
+    )
+    columns = lax.all_to_all(packed, ("gx", "gy"), split_axis=0, concat_axis=0)
+    place = lax.axis_index("gx") * sides + lax.axis_index("gy")
+    vmem = pl.BlockSpec(memory_space=pltpu.VMEM)
+    spectrum_shape = (RADIX, PART, groups * lanes)
+    main, extra = call(
+        columns_kernel,
+        [spectrum_shape, spectrum_shape],
+        [(RADIX, PART, 2 * groups * lanes)],
+        in_specs=[pl.BlockSpec(memory_space=pltpu.SMEM), vmem, vmem],
+        operands=(place.astype(jnp.int32).reshape(1), columns, across),
+    )
+    results = []
+    for begin, end in CHUNKS:
+        numbers = tuple(range(begin, end))
+        pair_count = min(2 * end, len(PAIRS)) - 2 * begin
+        (crossed,) = call(
+            functools.partial(pairs_kernel, numbers),
+            [(devices, len(numbers), rows, lanes)],
+            [(RADIX, PART, len(numbers) * lanes)],
+            operands=(main, extra, across_back),
+        )
+        rows_of = lax.all_to_all(crossed, ("gx", "gy"), split_axis=0, concat_axis=0)
+        (real_rows,) = call(
+            functools.partial(back_kernel, pair_count),
+            [(sides, pair_count, rows, cols)],
+            [(pair_count * rows, GRID)],
+            operands=(rows_of, small_back, large_back),
+        )
+        swapped = lax.all_to_all(real_rows, "gy", split_axis=0, concat_axis=0)
+        results.append(
+            jnp.transpose(swapped, (1, 0, 2, 3)).reshape(pair_count, 1, row_count, cols)
+        )
+    return jnp.concatenate(results, axis=0)
+
+
+def fits_pencils(mesh):
+    devices = mesh.shape["gx"] * mesh.shape["gy"]
+    return devices * 2 * KEEP == GRID and GRID // mesh.shape["gy"] % PART == 0
+
+
 def solution(mesh):
     in_specs = (
         P(None, "gx", "gy"),
@@ -173,5 +552,6 @@
         P(None, "gx", "gy"),
         P(None, None, "gx", "gy"),
     )
+    local = pencil_local if fits_pencils(mesh) else plain_local
     out_specs = P(None, None, "gx", "gy")
     return jax.shard_map(local, mesh=mesh, in_specs=in_specs, out_specs=out_specs, check_vma=False)

time: 1620 us -> 604 us (0.37)
  blocking collectives: 803 us -> 116 us
  local copies, waits for them, and re-layouts: 361 us -> 12.3 us
  matrix products: 203 us -> 0 us
  waiting for transfers between devices: 127 us -> 293 us
  Pallas kernels: 0 us -> 146 us
  other arithmetic: 101 us -> 8.09 us
    all_to_all x4 -> x2, blocking collectives: 803 us -> 116 us  [the longest x1 74.9 us: pencil_local(): rows_of = lax.all_to_all(crossed, ('gx', 'gy'), split_axis=0, concat_axis=0)]
    dot_general x30 -> x0, matrix products: 203 us -> none  [product(): jnp.einsum(pattern, values, matrix, precision=HIGHEST, preferred_element_...]
    all_to_all x2 -> x6, waiting for transfers between devices: 127 us -> 293 us  [the longest x2 146 us: pencil_local(): rows_of = lax.all_to_all(crossed, ('gx', 'gy'), split_axis=0, concat_axis=0)]
    pallas_call x0 -> x8, Pallas kernels: none -> 146 us  [call(): pl.pallas_call(body, out_shape=[jax.ShapeDtypeStruct(shape, jnp.float32)...]
    another operation x13 -> x0, local copies, waits for them, and re-layouts: 136 us -> none  [the longest x9 103 us: contract(): jnp.stack([product(real_part, cosine) - product(imag_part, sine_part), pr...]
    unnamed x34 -> x6, local copies, waits for them, and re-layouts: 86.8 us -> 3.28 us
    slice x9 -> x0, local copies, waits for them, and re-layouts: 74.6 us -> none  [the longest x5 35 us: contract(): real_part, imag_part = (stacked[0], stacked[1])]
    another operation x8 -> x0, other arithmetic: 42.4 us -> none  [the longest x4 30.3 us: contract(): jnp.stack([product(real_part, cosine) - product(imag_part, sine_part), pr...]
  transfers between devices with their start and end apart: 2 -> 6, of which waited for: 2 -> 6; matrix products, arithmetic and copies ran while one was open for 0% -> 1% of each run, Pallas kernels for 0% -> 14%
where the time goes in v1:
time: 604 us
  waiting for transfers between devices  293 us (49%)
  Pallas kernels  146 us (24%)
  blocking collectives  116 us (19%)
  starting transfers between devices  27.8 us (5%)
  local copies, waits for them, and re-layouts  12.3 us (2%)
  other arithmetic  8.09 us (1%)
    all_to_all x2, waiting for transfers between devices, pencil_local(): rows_of = lax.all_to_all(crossed, ('gx', 'gy'), split_axis=0, concat_axis=0)  146 us
    pallas_call x8, Pallas kernels, call(): pl.pallas_call(body, out_shape=[jax.ShapeDtypeStruct(shape, jnp.float32)...  146 us
    all_to_all x3, waiting for transfers between devices, pencil_local(): swapped = lax.all_to_all(real_rows, 'gy', split_axis=0, concat_axis=0)  75.3 us
    all_to_all x1, blocking collectives, pencil_local(): rows_of = lax.all_to_all(crossed, ('gx', 'gy'), split_axis=0, concat_axis=0)  74.9 us
    all_to_all x1, waiting for transfers between devices, pencil_local(): columns = lax.all_to_all(packed, ('gx', 'gy'), split_axis=0, concat_axis=0)  71.3 us
    all_to_all x1, blocking collectives, pencil_local(): lines = lax.all_to_all(sent, 'gy', split_axis=0, concat_axis=0)  41.1 us
    all_to_all x3, starting transfers between devices, pencil_local(): swapped = lax.all_to_all(real_rows, 'gy', split_axis=0, concat_axis=0)  15.3 us
  transfers between devices with their start and end apart: 6, of which 6 were waited for; matrix products, arithmetic and copies ran while one was open for 1% of the time, Pallas kernels for 14%

profile of v1, /device:TPU:0, one launch (start us, length us, event | category | flops | bytes accessed | tf_op | source)
XLA Modules:
  0.0 603.5 jit_solution(2403018283959745773)
XLA Ops:
  0.0 1.1 convert_add_fusion
  1.1 2.1 maximum_bitcast_fusion.1
  3.2 41.1 %all_to_all.40.x_ref = f32[2,6,64,1024]{3,2,1,0:T(8,128)} all-to-all(f32[2,6,64,1024]{3,2,1,0:T(8,128)S(1)} %maximum_bitcast_fusion.1), channel_id=1, replica_groups=mesh['gx'=16,'gy'=2] {'gy'}, dimensions={0} | all-to-all | bytes 6291456 | tf_op jit(solution)/shard_map/all_to_all | solution.py:499
  44.4 7.4 %shard_map.100 = f32[32,3,64,128]{3,2,1,0:T(8,128)} custom-call(f32[2,6,64,1024]{3,2,1,0:T(8,128)} %all_to_all.40.x_ref, bf16[2,2,256,256]{3,2,1,0:T(8,128)(2,1)} %constant.25.clone.small_ref, bf16[2,3,512,512]{3,2,1,0:T(8,128)(2,1)} %constant.26.clone.large_ref), custom_call_target="tpu_custom_call" | custom-call | tf_op jit(solution)/shard_map/pallas_call | solution.py:480
  51.8 5.1 all-to-all-start.1
  56.9 71.3 %all-to-all-done.1.x_ref = f32[32,3,64,128]{3,2,1,0:T(8,128)S(1)} async-done(((f32[32,3,64,128]{3,2,1,0:T(8,128)}), f32[32,3,64,128]{3,2,1,0:T(8,128)S(1)}, u32[]{:S(2)}, u32[]{:S(2)}) %all-to-all-start.1) | async-done | bytes 3145760 | tf_op jit(solution)/shard_map/all_to_all | solution.py:508
  128.2 0.0 copy-start.1
  128.2 1.7 copy-done.1
  129.9 17.7 %shard_map.101 = (f32[8,256,384]{2,1,0:T(8,128)}, f32[8,256,384]{2,1,0:T(8,128)}) custom-call(s32[1]{0:T(128)} %bitcast.special_ref, f32[32,3,64,128]{3,2,1,0:T(8,128)} %copy-done.1, bf16[2,8,256,512]{3,2,1,0:T(8,128)(2,1)} %constant.29.clone.across_ref), custom_call_target="tpu_custom_call" | custom-call | tf_op jit(solution)/shard_map/pallas_call | solution.py:480
  147.6 26.4 %shard_map.106 = f32[32,3,64,128]{3,2,1,0:T(8,128)} custom-call(f32[8,256,384]{2,1,0:T(8,128)} %get-tuple-element.7.main_ref, f32[8,256,384]{2,1,0:T(8,128)} %get-tuple-element.8.extra_ref, bf16[2,8,256,512]{3,2,1,0:T(8,128)(2,1)} %constant.30.clone.back_ref), custom_call_target="tpu_custom_call" | custom-call | tf_op jit(solution)/shard_map/pallas_call | solution.py:480
  174.0 74.9 %all_to_all.41.x_ref = f32[32,3,64,128]{3,2,1,0:T(8,128)} all-to-all(f32[32,3,64,128]{3,2,1,0:T(8,128)} %shard_map.106), channel_id=1, replica_groups=mesh['gx'=16,'gy'=2] {'gx','gy'}, dimensions={0} | all-to-all | bytes 6291456 | tf_op jit(solution)/shard_map/all_to_all | solution.py:529
  248.9 9.4 %shard_map.107 = f32[2,5,64,1024]{3,2,1,0:T(8,128)} custom-call(f32[32,3,64,128]{3,2,1,0:T(8,128)} %all_to_all.41.x_ref, bf16[2,2,256,256]{3,2,1,0:T(8,128)(2,1)} %constant.27.clone.small_ref, bf16[2,3,512,512]{3,2,1,0:T(8,128)(2,1)} %constant.28.clone.large_ref), custom_call_target="tpu_custom_call" | custom-call | tf_op jit(solution)/shard_map/pallas_call | solution.py:480
  258.3 3.9 all-to-all-start.7
  262.2 29.9 %shard_map.102 = f32[32,4,64,128]{3,2,1,0:T(8,128)} custom-call(f32[8,256,384]{2,1,0:T(8,128)} %get-tuple-element.7.main_ref, f32[8,256,384]{2,1,0:T(8,128)} %get-tuple-element.8.extra_ref, bf16[2,8,256,512]{3,2,1,0:T(8,128)(2,1)} %constant.30.clone.back_ref), custom_call_target="tpu_custom_call" | custom-call | tf_op jit(solution)/shard_map/pallas_call | solution.py:480
  292.1 1.0 all-to-all-done.7
  293.1 3.6 all-to-all-start.2
  296.7 29.3 %shard_map.104 = f32[32,4,64,128]{3,2,1,0:T(8,128)} custom-call(f32[8,256,384]{2,1,0:T(8,128)} %get-tuple-element.7.main_ref, f32[8,256,384]{2,1,0:T(8,128)} %get-tuple-element.8.extra_ref, bf16[2,8,256,512]{3,2,1,0:T(8,128)(2,1)} %constant.30.clone.back_ref), custom_call_target="tpu_custom_call" | custom-call | tf_op jit(solution)/shard_map/pallas_call | solution.py:480
  325.9 65.2 %all-to-all-done.2.x_ref = f32[32,4,64,128]{3,2,1,0:T(8,128)} async-done(((f32[32,4,64,128]{3,2,1,0:T(8,128)}), f32[32,4,64,128]{3,2,1,0:T(8,128)}, u32[]{:S(2)}, u32[]{:S(2)}) %all-to-all-start.2) | async-done | bytes 4194336 | tf_op jit(solution)/shard_map/all_to_all | solution.py:529
  391.1 3.8 all-to-all-start.4
  394.9 13.1 %shard_map.103 = f32[2,8,64,1024]{3,2,1,0:T(8,128)} custom-call(f32[32,4,64,128]{3,2,1,0:T(8,128)} %all-to-all-done.2.x_ref, bf16[2,2,256,256]{3,2,1,0:T(8,128)(2,1)} %constant.27.clone.small_ref, bf16[2,3,512,512]{3,2,1,0:T(8,128)(2,1)} %constant.28.clone.large_ref), custom_call_target="tpu_custom_call" | custom-call | tf_op jit(solution)/shard_map/pallas_call | solution.py:480
  408.0 81.2 %all-to-all-done.4.x_ref = f32[32,4,64,128]{3,2,1,0:T(8,128)} async-done(((f32[32,4,64,128]{3,2,1,0:T(8,128)}), f32[32,4,64,128]{3,2,1,0:T(8,128)}, u32[]{:S(2)}, u32[]{:S(2)}) %all-to-all-start.4) | async-done | bytes 4194336 | tf_op jit(solution)/shard_map/all_to_all | solution.py:529
  489.1 5.8 all-to-all-start.3
  495.0 13.1 %shard_map.105 = f32[2,8,64,1024]{3,2,1,0:T(8,128)} custom-call(f32[32,4,64,128]{3,2,1,0:T(8,128)} %all-to-all-done.4.x_ref, bf16[2,2,256,256]{3,2,1,0:T(8,128)(2,1)} %constant.27.clone.small_ref, bf16[2,3,512,512]{3,2,1,0:T(8,128)(2,1)} %constant.28.clone.large_ref), custom_call_target="tpu_custom_call" | custom-call | tf_op jit(solution)/shard_map/pallas_call | solution.py:480
  508.1 34.1 %all-to-all-done.3 = f32[2,8,64,1024]{3,2,1,0:T(8,128)} async-done(((f32[2,8,64,1024]{3,2,1,0:T(8,128)}), f32[2,8,64,1024]{3,2,1,0:T(8,128)}, u32[]{:S(2)}, u32[]{:S(2)}) %all-to-all-start.3) | async-done | bytes 4194336 | tf_op jit(solution)/shard_map/all_to_all | solution.py:536
  542.2 5.6 all-to-all-start.5
  547.8 1.6 copy.14
  549.5 4.7 copy.12
  554.2 40.2 %all-to-all-done.5 = f32[2,8,64,1024]{3,2,1,0:T(8,128)} async-done(((f32[2,8,64,1024]{3,2,1,0:T(8,128)}), f32[2,8,64,1024]{3,2,1,0:T(8,128)}, u32[]{:S(2)}, u32[]{:S(2)}) %all-to-all-start.5) | async-done | bytes 4194336 | tf_op jit(solution)/shard_map/all_to_all | solution.py:536
  594.4 2.7 copy.13
  597.1 0.8 copy-done
  597.8 0.8 copy-done.2
  598.7 4.9 maximum_bitcast_fusion
  (2 shorter events, 0.0 us)
Async XLA Ops:
  51.8 76.4 %all-to-all-start.1 = ((f32[32,3,64,128]{3,2,1,0:T(8,128)}), f32[32,3,64,128]{3,2,1,0:T(8,128)S(1)}, u32[]{:S(2)}, u32[]{:S(2)}) async-start(f32[32,3,64,128]{3,2,1,0:T(8,128)} %shard_map.100), calls=%async_computation.1 | async-start | bytes 6291456 | tf_op jit(solution)/shard_map/all_to_all | solution.py:508
  128.2 1.7 copy-start.1
  258.3 34.7 %all-to-all-start.7 = ((f32[2,5,64,1024]{3,2,1,0:T(8,128)}), f32[2,5,64,1024]{3,2,1,0:T(8,128)S(1)}, u32[]{:S(2)}, u32[]{:S(2)}) async-start(f32[2,5,64,1024]{3,2,1,0:T(8,128)} %shard_map.107), calls=%async_computation.7 | async-start | bytes 5242880 | tf_op jit(solution)/shard_map/all_to_all | solution.py:536
  293.1 98.0 %all-to-all-start.2 = ((f32[32,4,64,128]{3,2,1,0:T(8,128)}), f32[32,4,64,128]{3,2,1,0:T(8,128)}, u32[]{:S(2)}, u32[]{:S(2)}) async-start(f32[32,4,64,128]{3,2,1,0:T(8,128)} %shard_map.102), calls=%async_computation.2 | async-start | bytes 8388608 | tf_op jit(solution)/shard_map/all_to_all | solution.py:529
  391.1 98.0 %all-to-all-start.4 = ((f32[32,4,64,128]{3,2,1,0:T(8,128)}), f32[32,4,64,128]{3,2,1,0:T(8,128)}, u32[]{:S(2)}, u32[]{:S(2)}) async-start(f32[32,4,64,128]{3,2,1,0:T(8,128)} %shard_map.104), calls=%async_computation.4 | async-start | bytes 8388608 | tf_op jit(solution)/shard_map/all_to_all | solution.py:529
  489.1 53.1 %all-to-all-start.3 = ((f32[2,8,64,1024]{3,2,1,0:T(8,128)}), f32[2,8,64,1024]{3,2,1,0:T(8,128)}, u32[]{:S(2)}, u32[]{:S(2)}) async-start(f32[2,8,64,1024]{3,2,1,0:T(8,128)} %shard_map.103), calls=%async_computation.3 | async-start | bytes 8388608 | tf_op jit(solution)/shard_map/all_to_all | solution.py:536
  542.2 52.2 %all-to-all-start.5 = ((f32[2,8,64,1024]{3,2,1,0:T(8,128)}), f32[2,8,64,1024]{3,2,1,0:T(8,128)}, u32[]{:S(2)}, u32[]{:S(2)}) async-start(f32[2,8,64,1024]{3,2,1,0:T(8,128)} %shard_map.105), calls=%async_computation.5 | async-start | bytes 8388608 | tf_op jit(solution)/shard_map/all_to_all | solution.py:536
  594.4 3.4 copy-start
  594.4 4.3 copy-start.2

commit v2 on v1

--- a/solution.py
+++ b/solution.py
@@ -177,7 +177,12 @@
 KEEP = 32
 ROOT = math.sqrt(0.5)
 PAIRS = [(i, j) for i in range(FIELD_COUNT) for j in range(i, FIELD_COUNT)]
-CHUNKS = ((0, 4), (4, 8), (8, 11))
+CHUNKS = (
+    (PAIRS[0:4],),
+    (PAIRS[6:9], PAIRS[11:13], PAIRS[15:16]),
+    (PAIRS[4:6], PAIRS[9:11], PAIRS[13:15]),
+    (PAIRS[16:21],),
+)
 VMEM_BYTES = 56 * 1024 * 1024
 
 
@@ -375,17 +380,20 @@
     )
 
 
-def pairs_kernel(numbers, main_ref, extra_ref, back_ref, out_ref, spread):
+def pairs_kernel(pairs, used, *refs):
+    back_ref, out_ref, spread = refs[-3:]
+    main_refs = {group: refs[2 * n] for n, group in enumerate(used)}
+    extra_refs = {group: refs[2 * n + 1] for n, group in enumerate(used)}
     lanes = 4 * KEEP
     tile = 32
+    groups = (len(pairs) + 1) // 2
 
     def forms(ref, k1, rows, field):
-        group, side = field // 2, field % 2
-        value = ref[k1, rows, group * lanes : (group + 1) * lanes]
+        value = ref[k1, rows, :]
         shape = value.shape
         turned = pltpu.roll(value, 2 * KEEP, 1)
         low = lane_mask(shape, lanes, 2 * KEEP)
-        full = jnp.where(low, value, turned) if side == 0 else jnp.where(low, turned, value)
+        full = jnp.where(low, value, turned) if field % 2 == 0 else jnp.where(low, turned, value)
         forward, backward = pltpu.roll(full, lanes - KEEP, 1), pltpu.roll(full, KEEP, 1)
         real_lane = lane_mask(shape, 2 * KEEP, KEEP)
         real_part = jnp.where(real_lane, full, backward)
@@ -393,26 +401,25 @@
         turned_part = jnp.where(real_lane, forward, -backward)
         return real_part, imag_part, full, turned_part
 
-    used = [PAIRS[n] for q in numbers for n in (2 * q, 2 * q + 1) if n < len(PAIRS)]
-    fields = sorted({f for pair in used for f in pair})
+    fields = sorted({f for pair in pairs for f in pair})
 
     @pl.loop(0, RADIX)
     def _(k1):
         @pl.loop(0, PART // tile)
         def _(piece):
             rows = pl.ds(pl.multiple_of(piece * tile, tile), tile)
-            main = {f: forms(main_ref, k1, rows, f) for f in fields}
-            extra = {f: forms(extra_ref, k1, rows, f) for f in fields}
+            main = {f: forms(main_refs[f // 2], k1, rows, f) for f in fields}
+            extra = {f: forms(extra_refs[f // 2], k1, rows, f) for f in fields}
             low = lane_mask((tile, lanes), lanes, 2 * KEEP)
 
             def cross(n):
-                i, j = PAIRS[n]
+                i, j = pairs[n]
                 value = main[i][0] * main[j][2] + main[i][1] * main[j][3]
                 return value + (extra[i][1] * extra[j][2] - extra[i][0] * extra[j][3])
 
-            for place, q in enumerate(numbers):
-                one = cross(2 * q)
-                two = cross(2 * q + 1) if 2 * q + 1 < len(PAIRS) else jnp.zeros_like(one)
+            for place in range(groups):
+                one = cross(2 * place)
+                two = cross(2 * place + 1) if 2 * place + 1 < len(pairs) else jnp.zeros_like(one)
                 value = jnp.where(low, one, two)
                 spread[k1, rows, place * lanes : (place + 1) * lanes] = value
 
@@ -425,7 +432,7 @@
     @pl.loop(0, PART // tile)
     def _(piece):
         rows = pl.ds(pl.multiple_of(piece * tile, tile), tile)
-        for place in range(len(numbers)):
+        for place in range(groups):
             parts = [
                 spread[k1, rows, place * lanes : (place + 1) * lanes] for k1 in range(RADIX)
             ]
@@ -490,59 +497,89 @@
 def pencil_local(labels, damage, opening, strain):
     small, large, small_back, large_back, across, across_back = [jnp.asarray(t) for t in tables()]
     phase_field = labels.astype(jnp.float32) - 1.0
-    fields = jnp.concatenate([phase_field, damage, opening, strain[:, 0]], axis=0)
-    field_count, row_count, cols = fields.shape
+    row_count, cols = damage.shape[1:]
     sides = lax.axis_size("gy")
     devices = lax.axis_size("gx") * sides
     rows = row_count // sides
-    sent = jnp.transpose(fields.reshape(field_count, sides, rows, cols), (1, 0, 2, 3))
-    lines = lax.all_to_all(sent, "gy", split_axis=0, concat_axis=0)
-    groups = field_count // 2
     lanes = 4 * KEEP
-    (packed,) = call(
-        rows_kernel,
-        [(devices, groups, rows, lanes)],
-        [(field_count * rows, GRID)],
-        operands=(lines, small, large),
-    )
-    columns = lax.all_to_all(packed, ("gx", "gy"), split_axis=0, concat_axis=0)
-    place = lax.axis_index("gx") * sides + lax.axis_index("gy")
+    side = lax.axis_index("gy")
+    place = (lax.axis_index("gx") * sides + side).astype(jnp.int32).reshape(1)
     vmem = pl.BlockSpec(memory_space=pltpu.VMEM)
-    spectrum_shape = (RADIX, PART, groups * lanes)
-    main, extra = call(
-        columns_kernel,
-        [spectrum_shape, spectrum_shape],
-        [(RADIX, PART, 2 * groups * lanes)],
-        in_specs=[pl.BlockSpec(memory_space=pltpu.SMEM), vmem, vmem],
-        operands=(place.astype(jnp.int32).reshape(1), columns, across),
-    )
-    results = []
-    for begin, end in CHUNKS:
-        numbers = tuple(range(begin, end))
-        pair_count = min(2 * end, len(PAIRS)) - 2 * begin
+    swap = [(0, 1), (1, 0)]
+    couples = [
+        jnp.concatenate([phase_field, damage], axis=0),
+        jnp.concatenate([opening, strain[0]], axis=0),
+        strain[1:, 0],
+    ]
+    lines = []
+    for couple in couples:
+        kept = lax.dynamic_slice_in_dim(couple, side * rows, rows, axis=1)
+        sent = lax.dynamic_slice_in_dim(couple, (1 - side) * rows, rows, axis=1)
+        came = lax.ppermute(sent, "gy", swap)
+        lines.append(
+            jnp.stack([jnp.where(side == 0, kept, came), jnp.where(side == 0, came, kept)])
+        )
+    spectra = []
+    spectrum_shape = (RADIX, PART, lanes)
+    for line in lines:
+        (packed,) = call(
+            rows_kernel,
+            [(devices, 1, rows, lanes)],
+            [(2 * rows, GRID)],
+            operands=(line, small, large),
+        )
+        columns = lax.all_to_all(packed, ("gx", "gy"), split_axis=0, concat_axis=0)
+        spectra.append(
+            call(
+                columns_kernel,
+                [spectrum_shape, spectrum_shape],
+                [(RADIX, PART, 2 * lanes)],
+                in_specs=[pl.BlockSpec(memory_space=pltpu.SMEM), vmem, vmem],
+                operands=(place, columns, across),
+            )
+        )
+    crosses = []
+    for chunk in CHUNKS:
+        pairs = [pair for run in chunk for pair in run]
+        groups = (len(pairs) + 1) // 2
+        used = sorted({field // 2 for pair in pairs for field in pair})
         (crossed,) = call(
-            functools.partial(pairs_kernel, numbers),
-            [(devices, len(numbers), rows, lanes)],
-            [(RADIX, PART, len(numbers) * lanes)],
-            operands=(main, extra, across_back),
-        )
-        rows_of = lax.all_to_all(crossed, ("gx", "gy"), split_axis=0, concat_axis=0)
+            functools.partial(pairs_kernel, pairs, used),
+            [(devices, groups, rows, lanes)],
+            [(RADIX, PART, groups * lanes)],
+            operands=tuple(part for n in used for part in spectra[n]) + (across_back,),
+        )
+        crosses.append(crossed)
+    result = jnp.zeros((len(PAIRS), row_count, cols), jnp.float32)
+    for n, chunk in enumerate(CHUNKS):
+        pair_count = sum(len(run) for run in chunk)
+        rows_of = lax.all_to_all(crosses[n], ("gx", "gy"), split_axis=0, concat_axis=0)
         (real_rows,) = call(
             functools.partial(back_kernel, pair_count),
             [(sides, pair_count, rows, cols)],
             [(pair_count * rows, GRID)],
             operands=(rows_of, small_back, large_back),
         )
-        swapped = lax.all_to_all(real_rows, "gy", split_axis=0, concat_axis=0)
-        results.append(
-            jnp.transpose(swapped, (1, 0, 2, 3)).reshape(pair_count, 1, row_count, cols)
-        )
-    return jnp.concatenate(results, axis=0)
+        sent = lax.dynamic_index_in_dim(real_rows, 1 - side, 0, keepdims=False)
+        kept = lax.dynamic_index_in_dim(real_rows, side, 0, keepdims=False)
+        came = lax.ppermute(sent, "gy", swap)
+        if n + 2 < len(CHUNKS):
+            came, crosses[n + 2] = lax.optimization_barrier((came, crosses[n + 2]))
+        for half in range(2):
+            values = jnp.where(side == half, kept, came)
+            begin = 0
+            for run in chunk:
+                first = PAIRS.index(run[0])
+                result = lax.dynamic_update_slice(
+                    result, values[begin : begin + len(run)], (first, half * rows, 0)
+                )
+                begin += len(run)
+    return result.reshape(len(PAIRS), 1, row_count, cols)
 
 
 def fits_pencils(mesh):
     devices = mesh.shape["gx"] * mesh.shape["gy"]
-    return devices * 2 * KEEP == GRID and GRID // mesh.shape["gy"] % PART == 0
+    return devices * 2 * KEEP == GRID and mesh.shape["gy"] == 2
 
 
 def solution(mesh):

time: 604 us -> 482 us (0.80)
  blocking collectives: 116 us -> 0 us
  waiting for transfers between devices: 293 us -> 213 us
  Pallas kernels: 146 us -> 184 us
  local copies, waits for them, and re-layouts: 12.3 us -> 28.2 us
  starting transfers between devices: 27.8 us -> 42.1 us
    all_to_all x5 -> x4, waiting for transfers between devices: 222 us -> 40.2 us  [pencil_local(): lax.all_to_all(crosses[n], ('gx', 'gy'), split_axis=0, concat_axis=0)]
    ppermute x0 -> x7, waiting for transfers between devices: none -> 152 us  [pencil_local(): came = lax.ppermute(sent, 'gy', swap)]
    all_to_all x2 -> x0, blocking collectives: 116 us -> none  [the longest x1 74.9 us: pencil_local(): rows_of = lax.all_to_all(crossed, ('gx', 'gy'), split_axis=0, concat_axis=0)]
    all_to_all x1 -> x3, waiting for transfers between devices: 71.3 us -> 20.8 us  [pencil_local(): columns = lax.all_to_all(packed, ('gx', 'gy'), split_axis=0, concat_axis=0)]
    pallas_call x8 -> x14, Pallas kernels: 146 us -> 184 us  [call(): pl.pallas_call(body, out_shape=[jax.ShapeDtypeStruct(shape, jnp.float32)...]
    ppermute x0 -> x7, starting transfers between devices: none -> 10.1 us  [pencil_local(): came = lax.ppermute(sent, 'gy', swap)]
    dynamic_update_slice x0 -> x12, local copies, waits for them, and re-layouts: none -> 9.93 us  [pencil_local(): lax.dynamic_update_slice(result, values[begin:begin + len(run)], (first,...]
    all_to_all x1 -> x3, starting transfers between devices: 5.14 us -> 14.6 us  [pencil_local(): columns = lax.all_to_all(packed, ('gx', 'gy'), split_axis=0, concat_axis=0)]
  transfers between devices with their start and end apart: 6 -> 14, of which waited for: 6 -> 11; matrix products, arithmetic and copies ran while one was open for 1% -> 6% of each run, Pallas kernels for 14% -> 35%
where the time goes in v2:
time: 482 us; the launch traced here: 481 us
  waiting for transfers between devices  213 us (44%)
  Pallas kernels  184 us (38%)
  starting transfers between devices  42.1 us (9%)
  local copies, waits for them, and re-layouts  28.2 us (6%)
  other arithmetic  14 us (3%)
    pallas_call x14, Pallas kernels, call(): pl.pallas_call(body, out_shape=[jax.ShapeDtypeStruct(shape, jnp.float32)...  184 us
    ppermute x7, waiting for transfers between devices, pencil_local(): came = lax.ppermute(sent, 'gy', swap)  152 us
    all_to_all x4, waiting for transfers between devices, pencil_local(): lax.all_to_all(crosses[n], ('gx', 'gy'), split_axis=0, concat_axis=0)  40.2 us
    all_to_all x3, waiting for transfers between devices, pencil_local(): columns = lax.all_to_all(packed, ('gx', 'gy'), split_axis=0, concat_axis=0)  20.8 us
    all_to_all x4, starting transfers between devices, pencil_local(): lax.all_to_all(crosses[n], ('gx', 'gy'), split_axis=0, concat_axis=0)  17.4 us
    all_to_all x3, starting transfers between devices, pencil_local(): columns = lax.all_to_all(packed, ('gx', 'gy'), split_axis=0, concat_axis=0)  14.6 us
    ppermute x7, starting transfers between devices, pencil_local(): came = lax.ppermute(sent, 'gy', swap)  10.1 us
    dynamic_update_slice x12, local copies, waits for them, and re-layouts, pencil_local(): lax.dynamic_update_slice(result, values[begin:begin + len(run)], (first,...  9.93 us
  transfers between devices with their start and end apart: 14, of which 11 were waited for; matrix products, arithmetic and copies ran while one was open for 6% of the time, Pallas kernels for 35%

profile of v2, /device:TPU:0, one launch (start us, length us, event | category | flops | bytes accessed | tf_op | source)
XLA Modules:
  0.0 481.4 jit_solution(12031218539314887183)
XLA Ops:
  6.4 11.6 %collective-permute-done.1 = f32[2,64,1024]{2,1,0:T(8,128)} collective-permute-done((f32[2,64,1024]{2,1,0:T(8,128)S(1)}, f32[2,64,1024]{2,1,0:T(8,128)}, u32[]{:S(2)}, u32[]{:S(2)}) %collective-permute-start.1) | collective-permute-done | bytes 524320 | tf_op jit(solution)/shard_map/ppermute | solution.py:518
  18.1 10.4 %collective-permute-done = f32[2,64,1024]{2,1,0:T(8,128)} collective-permute-done((f32[2,64,1024]{2,1,0:T(8,128)S(1)}, f32[2,64,1024]{2,1,0:T(8,128)}, u32[]{:S(2)}, u32[]{:S(2)}) %collective-permute-start) | collective-permute-done | bytes 524320 | tf_op jit(solution)/shard_map/ppermute | solution.py:518
  30.9 4.4 shard_map.100
  35.3 6.1 %all-to-all-start = ((f32[32,1,64,128]{3,2,1,0:T(8,128)}), f32[32,1,64,128]{3,2,1,0:T(8,128)S(1)}, u32[]{:S(2)}, u32[]{:S(2)}) async-start(f32[32,1,64,128]{3,2,1,0:T(8,128)} %shard_map.100), calls=%async_computation | async-start | bytes 2097152 | tf_op jit(solution)/shard_map/all_to_all | solution.py:531
  42.4 4.4 shard_map.102
  46.8 20.8 %all-to-all-done.x_ref = f32[32,1,64,128]{3,2,1,0:T(8,128)S(1)} async-done(((f32[32,1,64,128]{3,2,1,0:T(8,128)}), f32[32,1,64,128]{3,2,1,0:T(8,128)S(1)}, u32[]{:S(2)}, u32[]{:S(2)}) %all-to-all-start) | async-done | bytes 1048608 | tf_op jit(solution)/shard_map/all_to_all | solution.py:531
  67.6 3.6 all-to-all-start.1
  74.5 21.8 %collective-permute-done.3 = f32[2,64,1024]{2,1,0:T(8,128)S(1)} collective-permute-done((f32[2,64,1024]{2,1,0:T(8,128)S(1)}, f32[2,64,1024]{2,1,0:T(8,128)S(1)}, u32[]{:S(2)}, u32[]{:S(2)}) %collective-permute-start.3) | collective-permute-done | bytes 524320 | tf_op jit(solution)/shard_map/ppermute | solution.py:518
  97.5 4.4 shard_map.106
  101.9 4.9 %all-to-all-start.3 = ((f32[32,1,64,128]{3,2,1,0:T(8,128)}), f32[32,1,64,128]{3,2,1,0:T(8,128)S(1)}, u32[]{:S(2)}, u32[]{:S(2)}) async-start(f32[32,1,64,128]{3,2,1,0:T(8,128)} %shard_map.106), calls=%async_computation.3 | async-start | bytes 2097152 | tf_op jit(solution)/shard_map/all_to_all | solution.py:531
  106.8 9.9 %shard_map.101 = (f32[8,256,128]{2,1,0:T(8,128)}, f32[8,256,128]{2,1,0:T(8,128)}) custom-call(s32[1]{0:T(128)} %bitcast.special_ref, f32[32,1,64,128]{3,2,1,0:T(8,128)} %copy-done.6, bf16[2,8,256,512]{3,2,1,0:T(8,128)(2,1)} %constant.94.clone.across_ref), custom_call_target="tpu_custom_call" | custom-call | tf_op jit(solution)/shard_map/pallas_call | solution.py:487
  116.6 9.9 %shard_map.103 = (f32[8,256,128]{2,1,0:T(8,128)}, f32[8,256,128]{2,1,0:T(8,128)}) custom-call(s32[1]{0:T(128)} %bitcast.special_ref, f32[32,1,64,128]{3,2,1,0:T(8,128)} %copy-done.8, bf16[2,8,256,512]{3,2,1,0:T(8,128)(2,1)} %constant.94.clone.across_ref), custom_call_target="tpu_custom_call" | custom-call | tf_op jit(solution)/shard_map/pallas_call | solution.py:487
  126.5 23.7 %shard_map.104 = f32[32,2,64,128]{3,2,1,0:T(8,128)} custom-call(f32[8,256,128]{2,1,0:T(8,128)} %get-tuple-element.15.refs_0_, f32[8,256,128]{2,1,0:T(8,128)} %get-tuple-element.16.refs_1_, f32[8,256,128]{2,1,0:T(8,128)} %get-tuple-element.17.refs_2_.refs_0_, f32[8,256,128]{2,1,0:T(8,128)} %get-tuple-element.18.refs_3_.refs_1_, ...), custom_call_target="tpu_custom_call" | custom-call | tf_op jit(solution)/shard_map/pallas_call | solution.py:487
  151.2 5.8 %all-to-all-start.2 = ((f32[32,2,64,128]{3,2,1,0:T(8,128)}), f32[32,2,64,128]{3,2,1,0:T(8,128)S(1)}, u32[]{:S(2)}, u32[]{:S(2)}) async-start(f32[32,2,64,128]{3,2,1,0:T(8,128)} %shard_map.104), calls=%async_computation.2 | async-start | bytes 4194304 | tf_op jit(solution)/shard_map/all_to_all | solution.py:556
  157.0 25.4 %shard_map.109 = f32[32,3,64,128]{3,2,1,0:T(8,128)} custom-call(f32[8,256,128]{2,1,0:T(8,128)} %get-tuple-element.15.refs_0_, f32[8,256,128]{2,1,0:T(8,128)} %get-tuple-element.16.refs_1_, f32[8,256,128]{2,1,0:T(8,128)} %get-tuple-element.17.refs_2_.refs_0_, f32[8,256,128]{2,1,0:T(8,128)} %get-tuple-element.18.refs_3_.refs_1_, ...), custom_call_target="tpu_custom_call" | custom-call | tf_op jit(solution)/shard_map/pallas_call | solution.py:487
  182.4 23.4 %all-to-all-done.2.x_ref = f32[32,2,64,128]{3,2,1,0:T(8,128)S(1)} async-done(((f32[32,2,64,128]{3,2,1,0:T(8,128)}), f32[32,2,64,128]{3,2,1,0:T(8,128)S(1)}, u32[]{:S(2)}, u32[]{:S(2)}) %all-to-all-start.2) | async-done | bytes 2097184 | tf_op jit(solution)/shard_map/all_to_all | solution.py:556
  207.1 3.8 all-to-all-start.4
  211.0 8.0 %shard_map.105 = f32[2,4,64,1024]{3,2,1,0:T(8,128)} custom-call(f32[32,2,64,128]{3,2,1,0:T(8,128)} %copy-done.5, bf16[2,2,256,256]{3,2,1,0:T(8,128)(2,1)} %constant.92.clone.small_ref, bf16[2,3,512,512]{3,2,1,0:T(8,128)(2,1)} %constant.93.clone.large_ref), custom_call_target="tpu_custom_call" | custom-call | tf_op jit(solution)/shard_map/pallas_call | solution.py:487
  221.9 9.8 %shard_map.107 = (f32[8,256,128]{2,1,0:T(8,128)}, f32[8,256,128]{2,1,0:T(8,128)}) custom-call(s32[1]{0:T(128)} %bitcast.special_ref, f32[32,1,64,128]{3,2,1,0:T(8,128)} %copy-done.7, bf16[2,8,256,512]{3,2,1,0:T(8,128)(2,1)} %constant.94.clone.across_ref), custom_call_target="tpu_custom_call" | custom-call | tf_op jit(solution)/shard_map/pallas_call | solution.py:487
  231.8 27.9 %shard_map.108 = f32[32,3,64,128]{3,2,1,0:T(8,128)} custom-call(f32[8,256,128]{2,1,0:T(8,128)} %get-tuple-element.15.refs_0_, f32[8,256,128]{2,1,0:T(8,128)} %get-tuple-element.16.refs_1_, f32[8,256,128]{2,1,0:T(8,128)} %get-tuple-element.17.refs_2_.refs_0_, f32[8,256,128]{2,1,0:T(8,128)} %get-tuple-element.18.refs_3_.refs_1_, ...), custom_call_target="tpu_custom_call" | custom-call | tf_op jit(solution)/shard_map/pallas_call | solution.py:487
  259.7 6.6 %collective-permute-done.2 = f32[4,64,1024]{2,1,0:T(8,128)} collective-permute-done((f32[4,64,1024]{2,1,0:T(8,128)S(1)}, f32[4,64,1024]{2,1,0:T(8,128)}, u32[]{:S(2)}, u32[]{:S(2)}) %collective-permute-start.2) | collective-permute-done | bytes 1048608 | tf_op jit(solution)/shard_map/ppermute | solution.py:565
  266.3 15.8 %all-to-all-done.4.x_ref = f32[32,3,64,128]{3,2,1,0:T(8,128)S(1)} async-done(((f32[32,3,64,128]{3,2,1,0:T(8,128)}), f32[32,3,64,128]{3,2,1,0:T(8,128)S(1)}, u32[]{:S(2)}, u32[]{:S(2)}) %all-to-all-start.4) | async-done | bytes 3145760 | tf_op jit(solution)/shard_map/all_to_all | solution.py:556
  283.8 3.7 all-to-all-start.5
  287.5 10.6 %shard_map.110 = f32[2,6,64,1024]{3,2,1,0:T(8,128)} custom-call(f32[32,3,64,128]{3,2,1,0:T(8,128)} %copy-done.2, bf16[2,2,256,256]{3,2,1,0:T(8,128)(2,1)} %constant.92.clone.small_ref, bf16[2,3,512,512]{3,2,1,0:T(8,128)(2,1)} %constant.93.clone.large_ref), custom_call_target="tpu_custom_call" | custom-call | tf_op jit(solution)/shard_map/pallas_call | solution.py:487
  301.5 25.6 %shard_map.111 = f32[32,3,64,128]{3,2,1,0:T(8,128)} custom-call(f32[8,256,128]{2,1,0:T(8,128)} %get-tuple-element.17.refs_2_.refs_0_, f32[8,256,128]{2,1,0:T(8,128)} %get-tuple-element.18.refs_3_.refs_1_, f32[8,256,128]{2,1,0:T(8,128)} %get-tuple-element.19.refs_4_.refs_2_, f32[8,256,128]{2,1,0:T(8,128)} %get-tuple-element.20.refs_5_.refs_3_, ...), custom_call_target="tpu_custom_call" | custom-call | tf_op jit(solution)/shard_map/pallas_call | solution.py:487
  327.1 30.7 %collective-permute-done.4 = f32[6,64,1024]{2,1,0:T(8,128)} collective-permute-done((f32[6,64,1024]{2,1,0:T(8,128)S(1)}, f32[6,64,1024]{2,1,0:T(8,128)}, u32[]{:S(2)}, u32[]{:S(2)}) %collective-permute-start.4) | collective-permute-done | bytes 1572896 | tf_op jit(solution)/shard_map/ppermute | solution.py:565
  358.8 4.0 all-to-all-start.6
  362.9 5.7 %pad_bitcast_fusion = f32[21,1,128,1024]{3,2,1,0:T(8,128)} fusion(f32[4,64,1024]{2,1,0:T(8,128)S(1)} %bitcast_select_fusion.7), kind=kLoop, calls=%fused_computation | loop fusion | bytes 12058624 | tf_op jit(solution)/shard_map/reshape | solution.py:577
  371.0 10.5 %shard_map.112 = f32[2,6,64,1024]{3,2,1,0:T(8,128)} custom-call(f32[32,3,64,128]{3,2,1,0:T(8,128)} %all-to-all-done.5.x_ref, bf16[2,2,256,256]{3,2,1,0:T(8,128)(2,1)} %constant.92.clone.small_ref, bf16[2,3,512,512]{3,2,1,0:T(8,128)(2,1)} %constant.93.clone.large_ref), custom_call_target="tpu_custom_call" | custom-call | tf_op jit(solution)/shard_map/pallas_call | solution.py:487
  391.5 45.4 %collective-permute-done.5 = f32[6,64,1024]{2,1,0:T(8,128)S(1)} collective-permute-done((f32[6,64,1024]{2,1,0:T(8,128)S(1)}, f32[6,64,1024]{2,1,0:T(8,128)S(1)}, u32[]{:S(2)}, u32[]{:S(2)}) %collective-permute-start.5) | collective-permute-done | bytes 1572896 | tf_op jit(solution)/shard_map/ppermute | solution.py:565
  437.2 9.4 %shard_map.113 = f32[2,5,64,1024]{3,2,1,0:T(8,128)} custom-call(f32[32,3,64,128]{3,2,1,0:T(8,128)} %all-to-all-done.6.x_ref, bf16[2,2,256,256]{3,2,1,0:T(8,128)(2,1)} %constant.92.clone.small_ref, bf16[2,3,512,512]{3,2,1,0:T(8,128)(2,1)} %constant.93.clone.large_ref), custom_call_target="tpu_custom_call" | custom-call | tf_op jit(solution)/shard_map/pallas_call | solution.py:487
  453.2 25.6 %collective-permute-done.6 = f32[5,64,1024]{2,1,0:T(8,128)S(1)} collective-permute-done((f32[5,64,1024]{2,1,0:T(8,128)S(1)}, f32[5,64,1024]{2,1,0:T(8,128)S(1)}, u32[]{:S(2)}, u32[]{:S(2)}) %collective-permute-start.6) | collective-permute-done | bytes 1310752 | tf_op jit(solution)/shard_map/ppermute | solution.py:565
  (66 shorter events, 47.6 us)
Async XLA Ops:
  0.0 28.5 %copy-start.9 = (f32[1,128,1024]{2,1,0:T(8,128)S(1)}, f32[1,128,1024]{2,1,0:T(8,128)}, u32[]{:S(2)}) copy-start(f32[1,128,1024]{2,1,0:T(8,128)} %param.12) | copy-start | bytes 1572868
  0.0 6.3 %copy-start.10 = (f32[1,128,1024]{2,1,0:T(8,128)S(1)}, f32[1,128,1024]{2,1,0:T(8,128)}, u32[]{:S(2)}) copy-start(f32[1,128,1024]{2,1,0:T(8,128)} %param.11) | copy-start | bytes 1572868
  2.2 15.9 %collective-permute-start.1 = (f32[2,64,1024]{2,1,0:T(8,128)S(1)}, f32[2,64,1024]{2,1,0:T(8,128)}, u32[]{:S(2)}, u32[]{:S(2)}) collective-permute-start(f32[2,64,1024]{2,1,0:T(8,128)S(1)} %fusion.2), channel_id=1, source_target_pairs={{0,1},{1,0},{2,3},{3,2},{4,5},{5,4},{6,7},{7,6},{8,9},{9,8},{10,11... | collective-permute-start | bytes 1572872 | tf_op jit(solution)/shard_map/ppermute | solution.py:518
  6.4 22.1 %collective-permute-start = (f32[2,64,1024]{2,1,0:T(8,128)S(1)}, f32[2,64,1024]{2,1,0:T(8,128)}, u32[]{:S(2)}, u32[]{:S(2)}) collective-permute-start(f32[2,64,1024]{2,1,0:T(8,128)S(1)} %fusion.4), channel_id=1, source_target_pairs={{0,1},{1,0},{2,3},{3,2},{4,5},{5,4},{6,7},{7,6},{8,9},{9,8},{10,11... | collective-permute-start | bytes 1572872 | tf_op jit(solution)/shard_map/ppermute | solution.py:518
  35.3 32.3 %all-to-all-start = ((f32[32,1,64,128]{3,2,1,0:T(8,128)}), f32[32,1,64,128]{3,2,1,0:T(8,128)S(1)}, u32[]{:S(2)}, u32[]{:S(2)}) async-start(f32[32,1,64,128]{3,2,1,0:T(8,128)} %shard_map.100), calls=%async_computation | async-start | bytes 2097152 | tf_op jit(solution)/shard_map/all_to_all | solution.py:531
  67.6 28.7 %copy-start.6 = (f32[32,1,64,128]{3,2,1,0:T(8,128)}, f32[32,1,64,128]{3,2,1,0:T(8,128)S(1)}, u32[]{:S(2)}) copy-start(f32[32,1,64,128]{3,2,1,0:T(8,128)S(1)} %all-to-all-done.x_ref) | copy-start | bytes 3145732
  67.6 34.3 %all-to-all-start.1 = ((f32[32,1,64,128]{3,2,1,0:T(8,128)}), f32[32,1,64,128]{3,2,1,0:T(8,128)S(1)}, u32[]{:S(2)}, u32[]{:S(2)}) async-start(f32[32,1,64,128]{3,2,1,0:T(8,128)} %shard_map.102), calls=%async_computation.1 | async-start | bytes 2097152 | tf_op jit(solution)/shard_map/all_to_all | solution.py:531
  72.6 23.6 %collective-permute-start.3 = (f32[2,64,1024]{2,1,0:T(8,128)S(1)}, f32[2,64,1024]{2,1,0:T(8,128)S(1)}, u32[]{:S(2)}, u32[]{:S(2)}) collective-permute-start(f32[2,64,1024]{2,1,0:T(8,128)S(1)} %dynamic-slice_bitcast_fusion.4), channel_id=1, source_target_pairs={{0,1},{1,0},{2,3},{3,2},{4,5},{5,4},{6,7},{7,6},{8,9},{9,8},{10,11... | collective-permute-start | bytes 1572872 | tf_op jit(solution)/shard_map/ppermute | solution.py:518
  101.9 14.8 %copy-start.8 = (f32[32,1,64,128]{3,2,1,0:T(8,128)}, f32[32,1,64,128]{3,2,1,0:T(8,128)S(1)}, u32[]{:S(2)}) copy-start(f32[32,1,64,128]{3,2,1,0:T(8,128)S(1)} %all-to-all-done.1.x_ref) | copy-start | bytes 3145732
  101.9 48.3 %all-to-all-start.3 = ((f32[32,1,64,128]{3,2,1,0:T(8,128)}), f32[32,1,64,128]{3,2,1,0:T(8,128)S(1)}, u32[]{:S(2)}, u32[]{:S(2)}) async-start(f32[32,1,64,128]{3,2,1,0:T(8,128)} %shard_map.106), calls=%async_computation.3 | async-start | bytes 2097152 | tf_op jit(solution)/shard_map/all_to_all | solution.py:531
  150.2 1.0 copy-start.7
  151.2 54.6 %all-to-all-start.2 = ((f32[32,2,64,128]{3,2,1,0:T(8,128)}), f32[32,2,64,128]{3,2,1,0:T(8,128)S(1)}, u32[]{:S(2)}, u32[]{:S(2)}) async-start(f32[32,2,64,128]{3,2,1,0:T(8,128)} %shard_map.104), calls=%async_computation.2 | async-start | bytes 4194304 | tf_op jit(solution)/shard_map/all_to_all | solution.py:556
  205.7 1.4 copy-start.5
  207.1 75.0 %all-to-all-start.4 = ((f32[32,3,64,128]{3,2,1,0:T(8,128)}), f32[32,3,64,128]{3,2,1,0:T(8,128)S(1)}, u32[]{:S(2)}, u32[]{:S(2)}) async-start(f32[32,3,64,128]{3,2,1,0:T(8,128)} %shard_map.109), calls=%async_computation.4 | async-start | bytes 6291456 | tf_op jit(solution)/shard_map/all_to_all | solution.py:556
  220.3 46.0 %collective-permute-start.2 = (f32[4,64,1024]{2,1,0:T(8,128)S(1)}, f32[4,64,1024]{2,1,0:T(8,128)}, u32[]{:S(2)}, u32[]{:S(2)}) collective-permute-start(f32[4,64,1024]{2,1,0:T(8,128)S(1)} %dynamic-slice_bitcast_fusion.3), channel_id=1, source_target_pairs={{0,1},{1,0},{2,3},{3,2},{4,5},{5,4},{6,7},{7,6},{8,9},{9,8},{10,11... | collective-permute-start | bytes 3145736 | tf_op jit(solution)/shard_map/ppermute | solution.py:565
  282.1 1.7 copy-start.2
  283.8 75.0 %all-to-all-start.5 = ((f32[32,3,64,128]{3,2,1,0:T(8,128)}), f32[32,3,64,128]{3,2,1,0:T(8,128)}, u32[]{:S(2)}, u32[]{:S(2)}) async-start(f32[32,3,64,128]{3,2,1,0:T(8,128)} %shard_map.108), calls=%async_computation.5 | async-start | bytes 6291456 | tf_op jit(solution)/shard_map/all_to_all | solution.py:556
  299.7 58.1 %collective-permute-start.4 = (f32[6,64,1024]{2,1,0:T(8,128)S(1)}, f32[6,64,1024]{2,1,0:T(8,128)}, u32[]{:S(2)}, u32[]{:S(2)}) collective-permute-start(f32[6,64,1024]{2,1,0:T(8,128)S(1)} %dynamic-slice_bitcast_fusion.1), channel_id=1, source_target_pairs={{0,1},{1,0},{2,3},{3,2},{4,5},{5,4},{6,7},{7,6},{8,9},{9,8},{10,11... | collective-permute-start | bytes 4718600 | tf_op jit(solution)/shard_map/ppermute | solution.py:565
  327.1 35.7 %copy-start.1 = (f32[2,4,64,1024]{3,2,1,0:T(8,128)S(1)}, f32[2,4,64,1024]{3,2,1,0:T(8,128)}, u32[]{:S(2)}) copy-start(f32[2,4,64,1024]{3,2,1,0:T(8,128)} %shard_map.105) | copy-start | bytes 6291460
  358.8 78.5 %all-to-all-start.6 = ((f32[32,3,64,128]{3,2,1,0:T(8,128)}), f32[32,3,64,128]{3,2,1,0:T(8,128)}, u32[]{:S(2)}, u32[]{:S(2)}) async-start(f32[32,3,64,128]{3,2,1,0:T(8,128)} %shard_map.111), calls=%async_computation.6 | async-start | bytes 6291456 | tf_op jit(solution)/shard_map/all_to_all | solution.py:556
  381.5 3.2 copy-start.3
  383.2 53.7 %collective-permute-start.5 = (f32[6,64,1024]{2,1,0:T(8,128)S(1)}, f32[6,64,1024]{2,1,0:T(8,128)S(1)}, u32[]{:S(2)}, u32[]{:S(2)}) collective-permute-start(f32[6,64,1024]{2,1,0:T(8,128)S(1)} %dynamic-slice_bitcast_fusion), channel_id=1, source_target_pairs={{0,1},{1,0},{2,3},{3,2},{4,5},{5,4},{6,7},{7,6},{8,9},{9,8},{10,11... | collective-permute-start | bytes 4718600 | tf_op jit(solution)/shard_map/ppermute | solution.py:565
  386.6 50.3 %copy-start.4 = (f32[2,6,64,1024]{3,2,1,0:T(8,128)S(1)}, f32[2,6,64,1024]{3,2,1,0:T(8,128)}, u32[]{:S(2)}) copy-start(f32[2,6,64,1024]{3,2,1,0:T(8,128)} %shard_map.112) | copy-start | bytes 9437188
  448.1 30.7 %collective-permute-start.6 = (f32[5,64,1024]{2,1,0:T(8,128)S(1)}, f32[5,64,1024]{2,1,0:T(8,128)S(1)}, u32[]{:S(2)}, u32[]{:S(2)}) collective-permute-start(f32[5,64,1024]{2,1,0:T(8,128)S(1)} %dynamic-slice_bitcast_fusion.2), channel_id=1, source_target_pairs={{0,1},{1,0},{2,3},{3,2},{4,5},{5,4},{6,7},{7,6},{8,9},{9,8},{10,11... | collective-permute-start | bytes 3932168 | tf_op jit(solution)/shard_map/ppermute | solution.py:565
  448.2 30.6 %copy-start = (f32[2,5,64,1024]{3,2,1,0:T(8,128)S(1)}, f32[2,5,64,1024]{3,2,1,0:T(8,128)}, u32[]{:S(2)}) copy-start(f32[2,5,64,1024]{3,2,1,0:T(8,128)} %shard_map.113) | copy-start | bytes 7864324

commit v3 on v2

--- a/solution.py
+++ b/solution.py
@@ -179,9 +179,9 @@
 PAIRS = [(i, j) for i in range(FIELD_COUNT) for j in range(i, FIELD_COUNT)]
 CHUNKS = (
     (PAIRS[0:4],),
-    (PAIRS[6:9], PAIRS[11:13], PAIRS[15:16]),
-    (PAIRS[4:6], PAIRS[9:11], PAIRS[13:15]),
-    (PAIRS[16:21],),
+    (PAIRS[6:9], PAIRS[11:13], PAIRS[15:16], PAIRS[4:6]),
+    (PAIRS[9:11], PAIRS[13:15], PAIRS[16:18]),
+    (PAIRS[18:21],),
 )
 VMEM_BYTES = 56 * 1024 * 1024
 
@@ -528,6 +528,8 @@
             [(2 * rows, GRID)],
             operands=(line, small, large),
         )
+        if len(spectra) == 2:
+            spectra[0], packed = lax.optimization_barrier((spectra[0], packed))
         columns = lax.all_to_all(packed, ("gx", "gy"), split_axis=0, concat_axis=0)
         spectra.append(
             call(

time: 482 us -> 494 us (1.025)
  waiting for transfers between devices: 213 us -> 221 us
    ppermute x7, waiting for transfers between devices: 152 us -> 159 us  [pencil_local(): came = lax.ppermute(sent, 'gy', swap)]
    dynamic_update_slice x12 -> x14, local copies, waits for them, and re-layouts: 9.93 us -> 11.6 us  [pencil_local(): lax.dynamic_update_slice(result, values[begin:begin + len(run)], (first,...]
  transfers between devices with their start and end apart: 14 -> 14, of which waited for: 11 -> 10; matrix products, arithmetic and copies ran while one was open for 6% -> 7% of each run, Pallas kernels for 35% -> 35%
where the time goes in v3:
time: 494 us; the launch traced here: 493 us
  waiting for transfers between devices  221 us (45%)
  Pallas kernels  184 us (37%)
  starting transfers between devices  43.8 us (9%)
  local copies, waits for them, and re-layouts  29.3 us (6%)
  other arithmetic  14.5 us (3%)
    pallas_call x14, Pallas kernels, call(): pl.pallas_call(body, out_shape=[jax.ShapeDtypeStruct(shape, jnp.float32)...  184 us
    ppermute x7, waiting for transfers between devices, pencil_local(): came = lax.ppermute(sent, 'gy', swap)  159 us
    all_to_all x4, waiting for transfers between devices, pencil_local(): lax.all_to_all(crosses[n], ('gx', 'gy'), split_axis=0, concat_axis=0)  41.4 us
    all_to_all x3, waiting for transfers between devices, pencil_local(): columns = lax.all_to_all(packed, ('gx', 'gy'), split_axis=0, concat_axis=0)  20.8 us
    all_to_all x4, starting transfers between devices, pencil_local(): lax.all_to_all(crosses[n], ('gx', 'gy'), split_axis=0, concat_axis=0)  18.5 us
    all_to_all x3, starting transfers between devices, pencil_local(): columns = lax.all_to_all(packed, ('gx', 'gy'), split_axis=0, concat_axis=0)  14.6 us
    dynamic_update_slice x14, local copies, waits for them, and re-layouts, pencil_local(): lax.dynamic_update_slice(result, values[begin:begin + len(run)], (first,...  11.6 us
    ppermute x7, starting transfers between devices, pencil_local(): came = lax.ppermute(sent, 'gy', swap)  10.7 us
  transfers between devices with their start and end apart: 14, of which 10 were waited for; matrix products, arithmetic and copies ran while one was open for 7% of the time, Pallas kernels for 35%

profile of v3, /device:TPU:0, one launch (start us, length us, event | category | flops | bytes accessed | tf_op | source)
XLA Modules:
  0.0 493.2 jit_solution(7554948551313973643)
XLA Ops:
  7.4 10.7 %collective-permute-done.2 = f32[2,64,1024]{2,1,0:T(8,128)} collective-permute-done((f32[2,64,1024]{2,1,0:T(8,128)S(1)}, f32[2,64,1024]{2,1,0:T(8,128)}, u32[]{:S(2)}, u32[]{:S(2)}) %collective-permute-start.2) | collective-permute-done | bytes 524320 | tf_op jit(solution)/shard_map/ppermute | solution.py:518
  18.1 10.4 %collective-permute-done = f32[2,64,1024]{2,1,0:T(8,128)} collective-permute-done((f32[2,64,1024]{2,1,0:T(8,128)S(1)}, f32[2,64,1024]{2,1,0:T(8,128)}, u32[]{:S(2)}, u32[]{:S(2)}) %collective-permute-start) | collective-permute-done | bytes 524320 | tf_op jit(solution)/shard_map/ppermute | solution.py:518
  30.9 4.4 shard_map.100
  35.3 6.1 %all-to-all-start = ((f32[32,1,64,128]{3,2,1,0:T(8,128)}), f32[32,1,64,128]{3,2,1,0:T(8,128)S(1)}, u32[]{:S(2)}, u32[]{:S(2)}) async-start(f32[32,1,64,128]{3,2,1,0:T(8,128)} %shard_map.100), calls=%async_computation | async-start | bytes 2097152 | tf_op jit(solution)/shard_map/all_to_all | solution.py:533
  42.4 4.4 shard_map.103
  46.8 20.8 %all-to-all-done.x_ref = f32[32,1,64,128]{3,2,1,0:T(8,128)S(1)} async-done(((f32[32,1,64,128]{3,2,1,0:T(8,128)}), f32[32,1,64,128]{3,2,1,0:T(8,128)S(1)}, u32[]{:S(2)}, u32[]{:S(2)}) %all-to-all-start) | async-done | bytes 1048608 | tf_op jit(solution)/shard_map/all_to_all | solution.py:533
  67.6 3.6 all-to-all-start.1
  75.1 21.2 %collective-permute-done.1 = f32[2,64,1024]{2,1,0:T(8,128)} collective-permute-done((f32[2,64,1024]{2,1,0:T(8,128)}, f32[2,64,1024]{2,1,0:T(8,128)}, u32[]{:S(2)}, u32[]{:S(2)}) %collective-permute-start.1) | collective-permute-done | bytes 524320 | tf_op jit(solution)/shard_map/ppermute | solution.py:518
  98.5 4.4 shard_map.102
  102.9 9.9 %shard_map.101 = (f32[8,256,128]{2,1,0:T(8,128)}, f32[8,256,128]{2,1,0:T(8,128)}) custom-call(s32[1]{0:T(128)} %bitcast.special_ref, f32[32,1,64,128]{3,2,1,0:T(8,128)} %copy-done.5, bf16[2,8,256,512]{3,2,1,0:T(8,128)(2,1)} %constant.100.clone.across_ref), custom_call_target="tpu_custom_call" | custom-call | tf_op jit(solution)/shard_map/pallas_call | solution.py:487
  112.8 4.9 all-to-all-start.3
  117.7 9.9 %shard_map.104 = (f32[8,256,128]{2,1,0:T(8,128)}, f32[8,256,128]{2,1,0:T(8,128)}) custom-call(s32[1]{0:T(128)} %bitcast.special_ref, f32[32,1,64,128]{3,2,1,0:T(8,128)} %copy-done.6, bf16[2,8,256,512]{3,2,1,0:T(8,128)(2,1)} %constant.100.clone.across_ref), custom_call_target="tpu_custom_call" | custom-call | tf_op jit(solution)/shard_map/pallas_call | solution.py:487
  127.7 23.7 %shard_map.105 = f32[32,2,64,128]{3,2,1,0:T(8,128)} custom-call(f32[8,256,128]{2,1,0:T(8,128)} %get-tuple-element.20.refs_0_, f32[8,256,128]{2,1,0:T(8,128)} %get-tuple-element.21.refs_1_, f32[8,256,128]{2,1,0:T(8,128)} %get-tuple-element.22.refs_2_, f32[8,256,128]{2,1,0:T(8,128)} %get-tuple-element.23.refs_3_, ...), custom_call_target="tpu_custom_call" | custom-call | tf_op jit(solution)/shard_map/pallas_call | solution.py:487
  151.4 5.8 %all-to-all-start.2 = ((f32[32,2,64,128]{3,2,1,0:T(8,128)}), f32[32,2,64,128]{3,2,1,0:T(8,128)S(1)}, u32[]{:S(2)}, u32[]{:S(2)}) async-start(f32[32,2,64,128]{3,2,1,0:T(8,128)} %shard_map.105), calls=%async_computation.2 | async-start | bytes 4194304 | tf_op jit(solution)/shard_map/all_to_all | solution.py:558
  157.2 9.9 %shard_map.107 = (f32[8,256,128]{2,1,0:T(8,128)}, f32[8,256,128]{2,1,0:T(8,128)}) custom-call(s32[1]{0:T(128)} %bitcast.special_ref, f32[32,1,64,128]{3,2,1,0:T(8,128)} %copy-done.7, bf16[2,8,256,512]{3,2,1,0:T(8,128)(2,1)} %constant.100.clone.across_ref), custom_call_target="tpu_custom_call" | custom-call | tf_op jit(solution)/shard_map/pallas_call | solution.py:487
  167.1 30.1 %shard_map.109 = f32[32,4,64,128]{3,2,1,0:T(8,128)} custom-call(f32[8,256,128]{2,1,0:T(8,128)} %get-tuple-element.20.refs_0_, f32[8,256,128]{2,1,0:T(8,128)} %get-tuple-element.21.refs_1_, f32[8,256,128]{2,1,0:T(8,128)} %get-tuple-element.22.refs_2_, f32[8,256,128]{2,1,0:T(8,128)} %get-tuple-element.23.refs_3_, ...), custom_call_target="tpu_custom_call" | custom-call | tf_op jit(solution)/shard_map/pallas_call | solution.py:487
  197.2 8.7 %all-to-all-done.2.x_ref = f32[32,2,64,128]{3,2,1,0:T(8,128)S(1)} async-done(((f32[32,2,64,128]{3,2,1,0:T(8,128)}), f32[32,2,64,128]{3,2,1,0:T(8,128)S(1)}, u32[]{:S(2)}, u32[]{:S(2)}) %all-to-all-start.2) | async-done | bytes 2097184 | tf_op jit(solution)/shard_map/all_to_all | solution.py:558
  207.3 4.0 all-to-all-start.4
  211.3 8.0 %shard_map.106 = f32[2,4,64,1024]{3,2,1,0:T(8,128)} custom-call(f32[32,2,64,128]{3,2,1,0:T(8,128)} %copy-done.4, bf16[2,2,256,256]{3,2,1,0:T(8,128)(2,1)} %constant.98.clone.small_ref, bf16[2,3,512,512]{3,2,1,0:T(8,128)(2,1)} %constant.99.clone.large_ref), custom_call_target="tpu_custom_call" | custom-call | tf_op jit(solution)/shard_map/pallas_call | solution.py:487
  222.2 27.8 %shard_map.108 = f32[32,3,64,128]{3,2,1,0:T(8,128)} custom-call(f32[8,256,128]{2,1,0:T(8,128)} %get-tuple-element.20.refs_0_, f32[8,256,128]{2,1,0:T(8,128)} %get-tuple-element.21.refs_1_, f32[8,256,128]{2,1,0:T(8,128)} %get-tuple-element.22.refs_2_, f32[8,256,128]{2,1,0:T(8,128)} %get-tuple-element.23.refs_3_, ...), custom_call_target="tpu_custom_call" | custom-call | tf_op jit(solution)/shard_map/pallas_call | solution.py:487
  250.1 22.7 %collective-permute-done.3 = f32[4,64,1024]{2,1,0:T(8,128)S(1)} collective-permute-done((f32[4,64,1024]{2,1,0:T(8,128)S(1)}, f32[4,64,1024]{2,1,0:T(8,128)S(1)}, u32[]{:S(2)}, u32[]{:S(2)}) %collective-permute-start.3) | collective-permute-done | bytes 1048608 | tf_op jit(solution)/shard_map/ppermute | solution.py:567
  272.8 32.7 %all-to-all-done.4.x_ref = f32[32,4,64,128]{3,2,1,0:T(8,128)} async-done(((f32[32,4,64,128]{3,2,1,0:T(8,128)}), f32[32,4,64,128]{3,2,1,0:T(8,128)}, u32[]{:S(2)}, u32[]{:S(2)}) %all-to-all-start.4) | async-done | bytes 4194336 | tf_op jit(solution)/shard_map/all_to_all | solution.py:558
  305.5 3.5 all-to-all-start.5
  309.1 13.1 %shard_map.110 = f32[2,8,64,1024]{3,2,1,0:T(8,128)} custom-call(f32[32,4,64,128]{3,2,1,0:T(8,128)} %all-to-all-done.4.x_ref, bf16[2,2,256,256]{3,2,1,0:T(8,128)(2,1)} %constant.98.clone.small_ref, bf16[2,3,512,512]{3,2,1,0:T(8,128)(2,1)} %constant.99.clone.large_ref), custom_call_target="tpu_custom_call" | custom-call | tf_op jit(solution)/shard_map/pallas_call | solution.py:487
  327.0 20.9 %shard_map.111 = f32[32,2,64,128]{3,2,1,0:T(8,128)} custom-call(f32[8,256,128]{2,1,0:T(8,128)} %get-tuple-element.25.refs_4_.refs_0_, f32[8,256,128]{2,1,0:T(8,128)} %get-tuple-element.26.refs_5_.refs_1_, bf16[2,8,256,512]{3,2,1,0:T(8,128)(2,1)} %constant.101.clone.refs_4_.refs_6_.refs_2_), custom_call_target="tpu_custom_call" | custom-call | tf_op jit(solution)/shard_map/pallas_call | solution.py:487
  348.0 44.2 %collective-permute-done.4 = f32[8,64,1024]{2,1,0:T(8,128)} collective-permute-done((f32[8,64,1024]{2,1,0:T(8,128)}, f32[8,64,1024]{2,1,0:T(8,128)}, u32[]{:S(2)}, u32[]{:S(2)}) %collective-permute-start.4) | collective-permute-done | bytes 2097184 | tf_op jit(solution)/shard_map/ppermute | solution.py:567
  392.1 5.2 %all-to-all-start.6 = ((f32[32,2,64,128]{3,2,1,0:T(8,128)}), f32[32,2,64,128]{3,2,1,0:T(8,128)}, u32[]{:S(2)}, u32[]{:S(2)}) async-start(f32[32,2,64,128]{3,2,1,0:T(8,128)} %shard_map.111), calls=%async_computation.6 | async-start | bytes 4194304 | tf_op jit(solution)/shard_map/all_to_all | solution.py:558
  397.4 5.7 %pad_bitcast_fusion = f32[21,1,128,1024]{3,2,1,0:T(8,128)} fusion(f32[4,64,1024]{2,1,0:T(8,128)S(1)} %bitcast_select_fusion.5), kind=kLoop, calls=%fused_computation | loop fusion | bytes 12058624 | tf_op jit(solution)/shard_map/reshape | solution.py:579
  404.2 10.7 %shard_map.112 = f32[2,6,64,1024]{3,2,1,0:T(8,128)} custom-call(f32[32,3,64,128]{3,2,1,0:T(8,128)} %all-to-all-done.5.x_ref, bf16[2,2,256,256]{3,2,1,0:T(8,128)(2,1)} %constant.98.clone.small_ref, bf16[2,3,512,512]{3,2,1,0:T(8,128)(2,1)} %constant.99.clone.large_ref), custom_call_target="tpu_custom_call" | custom-call | tf_op jit(solution)/shard_map/pallas_call | solution.py:487
  426.6 35.0 %collective-permute-done.5 = f32[6,64,1024]{2,1,0:T(8,128)S(1)} collective-permute-done((f32[6,64,1024]{2,1,0:T(8,128)S(1)}, f32[6,64,1024]{2,1,0:T(8,128)S(1)}, u32[]{:S(2)}, u32[]{:S(2)}) %collective-permute-start.5) | collective-permute-done | bytes 1572896 | tf_op jit(solution)/shard_map/ppermute | solution.py:567
  463.8 6.9 %shard_map.113 = f32[2,3,64,1024]{3,2,1,0:T(8,128)} custom-call(f32[32,2,64,128]{3,2,1,0:T(8,128)} %all-to-all-done.6.x_ref, bf16[2,2,256,256]{3,2,1,0:T(8,128)(2,1)} %constant.98.clone.small_ref, bf16[2,3,512,512]{3,2,1,0:T(8,128)(2,1)} %constant.99.clone.large_ref), custom_call_target="tpu_custom_call" | custom-call | tf_op jit(solution)/shard_map/pallas_call | solution.py:487
  476.2 14.9 %collective-permute-done.6 = f32[3,64,1024]{2,1,0:T(8,128)S(1)} collective-permute-done((f32[3,64,1024]{2,1,0:T(8,128)S(1)}, f32[3,64,1024]{2,1,0:T(8,128)S(1)}, u32[]{:S(2)}, u32[]{:S(2)}) %collective-permute-start.6) | collective-permute-done | bytes 786464 | tf_op jit(solution)/shard_map/ppermute | solution.py:567
  (66 shorter events, 48.7 us)
Async XLA Ops:
  0.0 28.5 %copy-start.8 = (f32[1,128,1024]{2,1,0:T(8,128)S(1)}, f32[1,128,1024]{2,1,0:T(8,128)}, u32[]{:S(2)}) copy-start(f32[1,128,1024]{2,1,0:T(8,128)} %param.12) | copy-start | bytes 1572868
  0.0 28.5 %copy-start.9 = (f32[1,128,1024]{2,1,0:T(8,128)S(1)}, f32[1,128,1024]{2,1,0:T(8,128)}, u32[]{:S(2)}) copy-start(f32[1,128,1024]{2,1,0:T(8,128)} %param.11) | copy-start | bytes 1572868
  2.2 15.9 %collective-permute-start.2 = (f32[2,64,1024]{2,1,0:T(8,128)S(1)}, f32[2,64,1024]{2,1,0:T(8,128)}, u32[]{:S(2)}, u32[]{:S(2)}) collective-permute-start(f32[2,64,1024]{2,1,0:T(8,128)S(1)} %fusion.2), channel_id=1, source_target_pairs={{0,1},{1,0},{2,3},{3,2},{4,5},{5,4},{6,7},{7,6},{8,9},{9,8},{10,11... | collective-permute-start | bytes 1572872 | tf_op jit(solution)/shard_map/ppermute | solution.py:518
  7.3 21.2 %collective-permute-start = (f32[2,64,1024]{2,1,0:T(8,128)S(1)}, f32[2,64,1024]{2,1,0:T(8,128)}, u32[]{:S(2)}, u32[]{:S(2)}) collective-permute-start(f32[2,64,1024]{2,1,0:T(8,128)S(1)} %fusion.4), channel_id=1, source_target_pairs={{0,1},{1,0},{2,3},{3,2},{4,5},{5,4},{6,7},{7,6},{8,9},{9,8},{10,11... | collective-permute-start | bytes 1572872 | tf_op jit(solution)/shard_map/ppermute | solution.py:518
  35.3 32.3 %all-to-all-start = ((f32[32,1,64,128]{3,2,1,0:T(8,128)}), f32[32,1,64,128]{3,2,1,0:T(8,128)S(1)}, u32[]{:S(2)}, u32[]{:S(2)}) async-start(f32[32,1,64,128]{3,2,1,0:T(8,128)} %shard_map.100), calls=%async_computation | async-start | bytes 2097152 | tf_op jit(solution)/shard_map/all_to_all | solution.py:533
  67.6 30.9 %copy-start.5 = (f32[32,1,64,128]{3,2,1,0:T(8,128)}, f32[32,1,64,128]{3,2,1,0:T(8,128)S(1)}, u32[]{:S(2)}) copy-start(f32[32,1,64,128]{3,2,1,0:T(8,128)S(1)} %all-to-all-done.x_ref) | copy-start | bytes 3145732
  67.6 45.2 %all-to-all-start.1 = ((f32[32,1,64,128]{3,2,1,0:T(8,128)}), f32[32,1,64,128]{3,2,1,0:T(8,128)S(1)}, u32[]{:S(2)}, u32[]{:S(2)}) async-start(f32[32,1,64,128]{3,2,1,0:T(8,128)} %shard_map.103), calls=%async_computation.1 | async-start | bytes 2097152 | tf_op jit(solution)/shard_map/all_to_all | solution.py:533
  73.4 22.9 %collective-permute-start.1 = (f32[2,64,1024]{2,1,0:T(8,128)}, f32[2,64,1024]{2,1,0:T(8,128)}, u32[]{:S(2)}, u32[]{:S(2)}) collective-permute-start(f32[2,64,1024]{2,1,0:T(8,128)} %dynamic-slice_bitcast_fusion.4), channel_id=1, source_target_pairs={{0,1},{1,0},{2,3},{3,2},{4,5},{5,4},{6,7},{7,6},{8,9},{9,8},{10,11... | collective-permute-start | bytes 1572872 | tf_op jit(solution)/shard_map/ppermute | solution.py:518
  112.8 4.9 copy-start.6
  112.8 38.5 %all-to-all-start.3 = ((f32[32,1,64,128]{3,2,1,0:T(8,128)}), f32[32,1,64,128]{3,2,1,0:T(8,128)S(1)}, u32[]{:S(2)}, u32[]{:S(2)}) async-start(f32[32,1,64,128]{3,2,1,0:T(8,128)} %shard_map.102), calls=%async_computation.3 | async-start | bytes 2097152 | tf_op jit(solution)/shard_map/all_to_all | solution.py:533
  151.4 5.8 %copy-start.7 = (f32[32,1,64,128]{3,2,1,0:T(8,128)}, f32[32,1,64,128]{3,2,1,0:T(8,128)S(1)}, u32[]{:S(2)}) copy-start(f32[32,1,64,128]{3,2,1,0:T(8,128)S(1)} %all-to-all-done.3.x_ref) | copy-start | bytes 3145732
  151.4 54.6 %all-to-all-start.2 = ((f32[32,2,64,128]{3,2,1,0:T(8,128)}), f32[32,2,64,128]{3,2,1,0:T(8,128)S(1)}, u32[]{:S(2)}, u32[]{:S(2)}) async-start(f32[32,2,64,128]{3,2,1,0:T(8,128)} %shard_map.105), calls=%async_computation.2 | async-start | bytes 4194304 | tf_op jit(solution)/shard_map/all_to_all | solution.py:558
  205.9 1.4 copy-start.4
  207.3 98.2 %all-to-all-start.4 = ((f32[32,4,64,128]{3,2,1,0:T(8,128)}), f32[32,4,64,128]{3,2,1,0:T(8,128)}, u32[]{:S(2)}, u32[]{:S(2)}) async-start(f32[32,4,64,128]{3,2,1,0:T(8,128)} %shard_map.109), calls=%async_computation.4 | async-start | bytes 8388608 | tf_op jit(solution)/shard_map/all_to_all | solution.py:558
  220.6 52.2 %collective-permute-start.3 = (f32[4,64,1024]{2,1,0:T(8,128)S(1)}, f32[4,64,1024]{2,1,0:T(8,128)S(1)}, u32[]{:S(2)}, u32[]{:S(2)}) collective-permute-start(f32[4,64,1024]{2,1,0:T(8,128)S(1)} %dynamic-slice_bitcast_fusion.2), channel_id=1, source_target_pairs={{0,1},{1,0},{2,3},{3,2},{4,5},{5,4},{6,7},{7,6},{8,9},{9,8},{10,11... | collective-permute-start | bytes 3145736 | tf_op jit(solution)/shard_map/ppermute | solution.py:567
  305.5 86.6 %all-to-all-start.5 = ((f32[32,3,64,128]{3,2,1,0:T(8,128)}), f32[32,3,64,128]{3,2,1,0:T(8,128)}, u32[]{:S(2)}, u32[]{:S(2)}) async-start(f32[32,3,64,128]{3,2,1,0:T(8,128)} %shard_map.108), calls=%async_computation.5 | async-start | bytes 6291456 | tf_op jit(solution)/shard_map/all_to_all | solution.py:558
  325.3 66.8 %collective-permute-start.4 = (f32[8,64,1024]{2,1,0:T(8,128)}, f32[8,64,1024]{2,1,0:T(8,128)}, u32[]{:S(2)}, u32[]{:S(2)}) collective-permute-start(f32[8,64,1024]{2,1,0:T(8,128)} %dynamic-slice_bitcast_fusion), channel_id=1, source_target_pairs={{0,1},{1,0},{2,3},{3,2},{4,5},{5,4},{6,7},{7,6},{8,9},{9,8},{10,11... | collective-permute-start | bytes 6291464 | tf_op jit(solution)/shard_map/ppermute | solution.py:567
  348.0 49.3 %copy-start.1 = (f32[2,4,64,1024]{3,2,1,0:T(8,128)S(1)}, f32[2,4,64,1024]{3,2,1,0:T(8,128)}, u32[]{:S(2)}) copy-start(f32[2,4,64,1024]{3,2,1,0:T(8,128)} %shard_map.106) | copy-start | bytes 6291460
  392.1 71.7 %all-to-all-start.6 = ((f32[32,2,64,128]{3,2,1,0:T(8,128)}), f32[32,2,64,128]{3,2,1,0:T(8,128)}, u32[]{:S(2)}, u32[]{:S(2)}) async-start(f32[32,2,64,128]{3,2,1,0:T(8,128)} %shard_map.111), calls=%async_computation.6 | async-start | bytes 4194304 | tf_op jit(solution)/shard_map/all_to_all | solution.py:558
  404.2 13.7 %copy-start = (f32[2,8,64,1024]{3,2,1,0:T(8,128)S(1)}, f32[2,8,64,1024]{3,2,1,0:T(8,128)}, u32[]{:S(2)}) copy-start(f32[2,8,64,1024]{3,2,1,0:T(8,128)} %shard_map.110) | copy-start | bytes 12582916
  416.4 45.3 %collective-permute-start.5 = (f32[6,64,1024]{2,1,0:T(8,128)S(1)}, f32[6,64,1024]{2,1,0:T(8,128)S(1)}, u32[]{:S(2)}, u32[]{:S(2)}) collective-permute-start(f32[6,64,1024]{2,1,0:T(8,128)S(1)} %dynamic-slice_bitcast_fusion.1), channel_id=1, source_target_pairs={{0,1},{1,0},{2,3},{3,2},{4,5},{5,4},{6,7},{7,6},{8,9},{9,8},{10,11... | collective-permute-start | bytes 4718600 | tf_op jit(solution)/shard_map/ppermute | solution.py:567
  420.0 41.7 %copy-start.2 = (f32[2,6,64,1024]{3,2,1,0:T(8,128)S(1)}, f32[2,6,64,1024]{3,2,1,0:T(8,128)}, u32[]{:S(2)}) copy-start(f32[2,6,64,1024]{3,2,1,0:T(8,128)} %shard_map.112) | copy-start | bytes 9437188
  470.6 20.5 %copy-start.3 = (f32[2,3,64,1024]{3,2,1,0:T(8,128)S(1)}, f32[2,3,64,1024]{3,2,1,0:T(8,128)}, u32[]{:S(2)}) copy-start(f32[2,3,64,1024]{3,2,1,0:T(8,128)} %shard_map.113) | copy-start | bytes 4718596
  472.0 19.2 %collective-permute-start.6 = (f32[3,64,1024]{2,1,0:T(8,128)S(1)}, f32[3,64,1024]{2,1,0:T(8,128)S(1)}, u32[]{:S(2)}, u32[]{:S(2)}) collective-permute-start(f32[3,64,1024]{2,1,0:T(8,128)S(1)} %dynamic-slice_bitcast_fusion.3), channel_id=1, source_target_pairs={{0,1},{1,0},{2,3},{3,2},{4,5},{5,4},{6,7},{7,6},{8,9},{9,8},{10,11... | collective-permute-start | bytes 2359304 | tf_op jit(solution)/shard_map/ppermute | solution.py:567
